TPU v7x, 32 devices: a whole 2x2x4 slice. The times are simulated.
32 devices in a mesh: replica: 8 (over z, core), shard: 4 (over y, x).
Axes of the slice: x: 2, y: 2, z: 4, core: 2. Of those that a mesh axis runs over, the one named last changes fastest.
Arguments:
- tokens: bfloat16 [32, 864, 1024], P('replica', 'shard'), may hold values from -6 to 6
- counts: int32 [32, 4], P('replica'), may hold values from 1 to 216, 577 in all within a row
- w_qkv: bfloat16 [1024, 3072], P('shard'), may hold values from -0.1875 to 0.1875
- w_proj: bfloat16 [1024, 1024], P('shard'), may hold values from -0.5 to 0.5
- w_fc1: bfloat16 [1024, 4096], P('shard'), may hold values from -0.1875 to 0.1875
- w_fc2: bfloat16 [4096, 1024], P('shard'), may hold values from -0.09375 to 0.09375
- norm_gains: bfloat16 [2048], P('shard'), may hold values from 0.25 to 1.75
- biases: bfloat16 [10240], P('shard'), may hold values from -3 to 3
- grad_out: bfloat16 [32, 864, 1024], P('replica', 'shard'), may hold values from -6 to 6
Outputs:
- result: bfloat16 [32, 864, 1024], P('replica', 'shard')
- grad_tokens: float32 [32, 864, 1024], P('replica', 'shard')
- grad_w_qkv: float32 [1024, 3072], P('shard')
- grad_w_proj: float32 [1024, 1024], P('shard')
- grad_w_fc1: float32 [1024, 4096], P('shard')
- grad_w_fc2: float32 [4096, 1024], P('shard')
- grad_norm_gains: float32 [2048], P('shard')
- grad_biases: float32 [10240], P('shard')
Inputs may be any that keep to these rules, and one draw needn't show every extreme that they name: valid rows of each image on each device of the shard axis, the first ones of its 216 slots there; an image's counts sum to 577; in every draw some image has 216 valid rows on some device.
All inputs are finite; a program needn't handle non-finite values.
Results may differ from a plain program's by a relative error of at most 0.0079.
Values may be sent and summed in bfloat16 or wider, within the bound.
A program may use at most 320 MiB of HBM per device.

v0:
```python
import jax
import jax.numpy as jnp
from jax import lax
from jax.sharding import PartitionSpec as P

HEAD = 64


norm_eps = 1e-06
big_negative = -1e30


def layer_norm(values, norm_gain, norm_shift):
    centered = values - jnp.mean(values, axis=-1, keepdims=True)
    spread = jnp.mean(centered * centered, axis=-1, keepdims=True)
    return centered * lax.rsqrt(spread + norm_eps) * norm_gain + norm_shift


def exact_gelu(values):
    return jax.nn.gelu(values, approximate=False)


def rows_inner(left, right):
    return lax.dot_general(
        left, right, (((0,), (0,)), ((), ())), preferred_element_type=jnp.float32
    )


def times_transpose(left, right):
    return lax.dot_general(
        left, right, (((1,), (1,)), ((), ())), preferred_element_type=jnp.float32
    )


def pair_slice(source, column_start):
    piece = lax.dynamic_slice_in_dim(source, column_start, 2 * HEAD, 2)
    return piece.reshape(piece.shape[0], piece.shape[1], 2, HEAD)


def head_scores(queries, key_all, key_valid, column_start):
    scores = jnp.einsum(
        "bqhe,bkhe->bhqk",
        pair_slice(queries, column_start),
        pair_slice(key_all, column_start),
        preferred_element_type=jnp.float32,
    ) * HEAD ** (-0.5)
    return jnp.where(key_valid[:, None, None, :], scores, big_negative)


def join_pairs(stacked):
    moved = jnp.moveaxis(stacked, 0, 2)
    return moved.reshape(moved.shape[0], moved.shape[1], moved.shape[2] * moved.shape[3])


def attend_forward(queries, key_all, value_all, key_valid):
    pair_count = queries.shape[2] // (2 * HEAD)

    def one_pair(pair_index):
        column_start = pair_index * 2 * HEAD
        scores = head_scores(queries, key_all, key_valid, column_start)
        row_max = jnp.max(scores, axis=-1, keepdims=True)
        exp_scores = jnp.exp(scores - row_max)
        exp_total = jnp.sum(exp_scores, axis=-1, keepdims=True)
        attn_probs = (exp_scores / exp_total).astype(jnp.bfloat16)
        attended = jnp.einsum(
            "bhqk,bkhe->bqhe",
            attn_probs,
            pair_slice(value_all, column_start),
            preferred_element_type=jnp.float32,
        )
        flat_pair = attended.reshape(attended.shape[0], attended.shape[1], 2 * HEAD)
        return (flat_pair, (row_max + jnp.log(exp_total))[..., 0])

    attended, log_totals = lax.map(one_pair, jnp.arange(pair_count, dtype=jnp.int32))
    return (join_pairs(attended), log_totals)


def attend_backward(queries, key_all, value_all, key_valid, log_totals, grad_attended):
    pair_count = queries.shape[2] // (2 * HEAD)
    scale_factor = HEAD ** (-0.5)

    def one_pair(members):
        pair_index, log_pair = members
        column_start = pair_index * 2 * HEAD
        scores = head_scores(queries, key_all, key_valid, column_start)
        attn_probs = jnp.exp(scores - log_pair[..., None])
        grad_pair = pair_slice(grad_attended, column_start)
        grad_probs = jnp.einsum(
            "bqhe,bkhe->bhqk",
            grad_pair,
            pair_slice(value_all, column_start),
            preferred_element_type=jnp.float32,
        )
        row_inner = jnp.sum(attn_probs * grad_probs, axis=-1, keepdims=True)
        grad_scores = (attn_probs * (grad_probs - row_inner)).astype(jnp.bfloat16)
        grad_query = (
            jnp.einsum(
                "bhqk,bkhe->bqhe",
                grad_scores,
                pair_slice(key_all, column_start),
                preferred_element_type=jnp.float32,
            )
            * scale_factor
        )
        grad_key = (
            jnp.einsum(
                "bhqk,bqhe->bkhe",
                grad_scores,
                pair_slice(queries, column_start),
                preferred_element_type=jnp.float32,
            )
            * scale_factor
        )
        grad_value = jnp.einsum(
            "bhqk,bqhe->bkhe",
            attn_probs.astype(jnp.bfloat16),
            grad_pair,
            preferred_element_type=jnp.float32,
        )
        query_shape = (grad_query.shape[0], grad_query.shape[1], 2 * HEAD)
        key_shape = (grad_key.shape[0], grad_key.shape[1], 2 * HEAD)
        return (
            grad_query.reshape(query_shape),
            grad_key.reshape(key_shape),
            grad_value.reshape(key_shape),
        )

    grad_query, grad_key, grad_value = lax.map(
        one_pair, (jnp.arange(pair_count, dtype=jnp.int32), log_totals)
    )
    return (join_pairs(grad_query), join_pairs(grad_key), join_pairs(grad_value))


def per_device(tokens, counts, w_qkv, w_proj, w_fc1, w_fc2, norm_gains, biases, grad_out):
    images, slot_rows, model_width = tokens.shape
    shards = lax.axis_size("shard")
    shard_rank = lax.axis_index("shard")
    row_count = images * slot_rows
    shaped = (images, slot_rows, model_width)
    own_counts = lax.dynamic_slice_in_dim(counts, shard_rank, 1, 1)
    slot_index = jnp.arange(slot_rows, dtype=jnp.int32)
    row_valid = (slot_index[None, :] < own_counts).astype(jnp.float32).reshape(row_count, 1)
    key_index = jnp.arange(shards * slot_rows, dtype=jnp.int32) % slot_rows
    key_valid = key_index[None, :] < jnp.repeat(counts, slot_rows, axis=1)
    shard_args = (w_qkv, w_proj, w_fc1, w_fc2, norm_gains, biases)
    gathered = (
        lax.all_gather(shard_args[0], "shard", axis=0, tiled=True),
        lax.all_gather(shard_args[1], "shard", axis=0, tiled=True),
        lax.all_gather(shard_args[2], "shard", axis=0, tiled=True),
        lax.all_gather(shard_args[3], "shard", axis=0, tiled=True),
        lax.all_gather(shard_args[4], "shard", axis=0, tiled=True),
        lax.all_gather(shard_args[5], "shard", axis=0, tiled=True),
    )
    qkv_full, proj_full, fc1_full, fc2_full, gains_full, biases_full = gathered
    gains_wide = gains_full.astype(jnp.float32)
    biases_wide = biases_full.astype(jnp.float32)
    inputs = tokens.astype(jnp.float32).reshape(row_count, model_width)
    normed_wide, norm_one_back = jax.vjp(
        layer_norm, inputs, gains_wide[:model_width], biases_wide[:model_width]
    )
    normed_one = normed_wide.astype(jnp.bfloat16)
    mixed_rows = jnp.dot(normed_one, qkv_full, preferred_element_type=jnp.float32)
    queries = (mixed_rows[:, :model_width] + biases_wide[2 * model_width : 3 * model_width]).astype(
        jnp.bfloat16
    )
    key_rows = mixed_rows[:, model_width : 2 * model_width].astype(jnp.bfloat16)
    value_rows = (
        mixed_rows[:, 2 * model_width :] + biases_wide[3 * model_width : 4 * model_width]
    ).astype(jnp.bfloat16)
    queries = queries.reshape(shaped)
    key_all, value_all = (
        lax.all_gather(key_rows.reshape(shaped), "shard", axis=1, tiled=True),
        lax.all_gather(value_rows.reshape(shaped), "shard", axis=1, tiled=True),
    )
    attended, log_totals = attend_forward(queries, key_all, value_all, key_valid)
    attended = attended.reshape(row_count, model_width).astype(jnp.bfloat16)
    middle = (
        inputs
        + jnp.dot(attended, proj_full, preferred_element_type=jnp.float32)
        + biases_wide[4 * model_width : 5 * model_width]
    )
    normed_mid, norm_two_back = jax.vjp(
        layer_norm, middle, gains_wide[model_width:], biases_wide[model_width : 2 * model_width]
    )
    normed_two = normed_mid.astype(jnp.bfloat16)
    before = (
        jnp.dot(normed_two, fc1_full, preferred_element_type=jnp.float32)
        + biases_wide[6 * model_width :]
    )
    hidden_wide, gelu_back = jax.vjp(exact_gelu, before)
    hidden = hidden_wide.astype(jnp.bfloat16)
    outcome = (
        middle
        + jnp.dot(hidden, fc2_full, preferred_element_type=jnp.float32)
        + biases_wide[5 * model_width : 6 * model_width]
    ) * row_valid
    output = outcome.astype(jnp.bfloat16).reshape(shaped)
    gathered_back = (
        lax.all_gather(shard_args[0], "shard", axis=0, tiled=True),
        lax.all_gather(shard_args[1], "shard", axis=0, tiled=True),
        lax.all_gather(shard_args[2], "shard", axis=0, tiled=True),
        lax.all_gather(shard_args[3], "shard", axis=0, tiled=True),
        lax.all_gather(shard_args[4], "shard", axis=0, tiled=True),
        lax.all_gather(shard_args[5], "shard", axis=0, tiled=True),
    )
    qkv_back, proj_back, fc1_back, fc2_back, gains_back, biases_back = gathered_back
    grad_rows = grad_out.astype(jnp.float32).reshape(row_count, model_width) * row_valid
    grad_branch = grad_rows.astype(jnp.bfloat16)
    grad_fc2 = rows_inner(hidden, grad_branch)
    grad_out_bias = jnp.sum(grad_branch, axis=0, dtype=jnp.float32)
    grad_hidden = times_transpose(grad_branch, fc2_back)
    grad_before = gelu_back(grad_hidden)[0].astype(jnp.bfloat16)
    grad_fc1 = rows_inner(normed_two, grad_before)
    grad_hidden_bias = jnp.sum(grad_before, axis=0, dtype=jnp.float32)
    grad_normed_two = times_transpose(grad_before, fc1_back)
    grad_middle_norm, grad_gain_two, grad_shift_two = norm_two_back(grad_normed_two)
    grad_middle = grad_rows + grad_middle_norm
    grad_branch_one = grad_middle.astype(jnp.bfloat16)
    grad_proj = rows_inner(attended, grad_branch_one)
    grad_proj_bias = jnp.sum(grad_branch_one, axis=0, dtype=jnp.float32)
    grad_attended = times_transpose(grad_branch_one, proj_back).astype(jnp.bfloat16).reshape(shaped)
    key_back, value_back = (
        lax.all_gather(key_rows.reshape(shaped), "shard", axis=1, tiled=True),
        lax.all_gather(value_rows.reshape(shaped), "shard", axis=1, tiled=True),
    )
    grad_query, grad_key_all, grad_value_all = attend_backward(
        queries, key_back, value_back, key_valid, log_totals, grad_attended
    )
    grad_key, grad_value = (
        lax.psum_scatter(grad_key_all, "shard", scatter_dimension=1, tiled=True),
        lax.psum_scatter(grad_value_all, "shard", scatter_dimension=1, tiled=True),
    )
    grad_mixed = jnp.concatenate(
        [
            grad_query.reshape(row_count, model_width).astype(jnp.bfloat16),
            grad_key.reshape(row_count, model_width).astype(jnp.bfloat16),
            grad_value.reshape(row_count, model_width).astype(jnp.bfloat16),
        ],
        axis=1,
    )
    grad_qkv = rows_inner(normed_one, grad_mixed)
    column_sums = jnp.sum(grad_mixed, axis=0, dtype=jnp.float32)
    grad_normed_one = times_transpose(grad_mixed, qkv_back)
    grad_inputs_norm, grad_gain_one, grad_shift_one = norm_one_back(grad_normed_one)
    grad_tokens = (grad_middle + grad_inputs_norm).reshape(shaped)
    grad_gains = jnp.concatenate([grad_gain_one, grad_gain_two])
    grad_biases = jnp.concatenate(
        [
            grad_shift_one,
            grad_shift_two,
            column_sums[:model_width],
            column_sums[2 * model_width :],
            grad_proj_bias,
            grad_out_bias,
            grad_hidden_bias,
        ]
    )
    local_grads = (grad_qkv, grad_proj, grad_fc1, grad_fc2, grad_gains, grad_biases)
    group_grads = (
        lax.psum_scatter(local_grads[0], "shard", scatter_dimension=0, tiled=True),
        lax.psum_scatter(local_grads[1], "shard", scatter_dimension=0, tiled=True),
        lax.psum_scatter(local_grads[2], "shard", scatter_dimension=0, tiled=True),
        lax.psum_scatter(local_grads[3], "shard", scatter_dimension=0, tiled=True),
        lax.psum_scatter(local_grads[4], "shard", scatter_dimension=0, tiled=True),
        lax.psum_scatter(local_grads[5], "shard", scatter_dimension=0, tiled=True),
    )
    total_grads = lax.psum(
        (
            group_grads[0],
            group_grads[1],
            group_grads[2],
            group_grads[3],
            group_grads[4],
            group_grads[5],
        ),
        "replica",
    )
    return (output, grad_tokens) + tuple(total_grads)


def solution(mesh):
    in_specs = (
        P("replica", "shard", None),
        P("replica", None),
        P("shard", None),
        P("shard", None),
        P("shard", None),
        P("shard", None),
        P("shard"),
        P("shard"),
        P("replica", "shard", None),
    )
    out_specs = (
        P("replica", "shard", None),
        P("replica", "shard", None),
        P("shard", None),
        P("shard", None),
        P("shard", None),
        P("shard", None),
        P("shard"),
        P("shard"),
    )
    return jax.shard_map(
        per_device, mesh=mesh, in_specs=in_specs, out_specs=out_specs, check_vma=False
    )
```

profile of v0, /device:TPU:0, one launch (start us, length us, event | category | flops | bytes accessed | tf_op | source)
XLA Modules:
  0.0 1795.7 jit_solution(5209599367007802275)
XLA Ops:
  10.5 9.7 all-gather.1
  33.6 49.3 %all-gather.9.cloned.1.call-done = bf16[1024,3072]{1,0:T(8,128)(2,1)} async-done(((bf16[256,3072]{1,0:T(8,128)(2,1)}), bf16[1024,3072]{1,0:T(8,128)(2,1)}) %all-gather.9.cloned.1.call-update) | async-done | bytes 6291472 | tf_op jit(solution)/shard_map/all_gather | solution.py:147
  111.2 62.9 %all-gather.11.cloned.1.call-done = bf16[4,864,1024]{2,0,1:T(4,128)(2,1)} async-done(((bf16[4,216,1024]{2,0,1:T(4,128)(2,1)}), bf16[4,864,1024]{2,0,1:T(4,128)(2,1)}) %all-gather.11.cloned.1.call-update) | async-done | bytes 7077904 | tf_op jit(solution)/shard_map/all_gather | solution.py:173
  174.1 13.1 copy.33
  187.3 66.0 %all-gather.13.cloned.1.call-done = bf16[4,864,1024]{2,0,1:T(4,128)(2,1)} async-done(((bf16[4,216,1024]{2,0,1:T(4,128)(2,1)}), bf16[4,864,1024]{2,0,1:T(4,128)(2,1)}) %all-gather.13.cloned.1.call-update) | async-done | bytes 7077904 | tf_op jit(solution)/shard_map/all_gather | solution.py:172
  253.3 13.0 copy.35
  267.9 82.4 %while.32 = (s32[]{:T(128)}, bf16[8,4,216,128]{2,3,1,0:T(8,128)(2,1)}, f32[8,4,2,216]{3,2,1,0:T(2,128)}, s32[8]{0:T(128)S(1)}, bf16[4,864,1024]{1,2,0:T(8,128)(2...) while((s32[]{:T(128)}, ...), condition=%wide.region_5.6_spmd.clone, body=%wide.region_2.5_spmd.clone.sunk | while | flops 400123584 | bytes 24721808 | solution.py:74
  360.8 18.9 %all-gather.17.cloned.1.call-done = bf16[1024,4096]{1,0:T(8,128)(2,1)} async-done(((bf16[256,4096]{1,0:T(8,128)(2,1)}), bf16[1024,4096]{1,0:T(8,128)(2,1)}) %all-gather.17.cloned.1.call-update) | async-done | bytes 8388624 | tf_op jit(solution)/shard_map/all_gather | solution.py:149
  379.7 13.9 fusion.43
  393.6 75.5 %all-gather.19.cloned.1.call-done = bf16[4096,1024]{1,0:T(8,128)(2,1)} async-done(((bf16[1024,1024]{1,0:T(8,128)(2,1)}), bf16[4096,1024]{1,0:T(8,128)(2,1)}) %all-gather.19.cloned.1.call-update) | async-done | bytes 8388624 | tf_op jit(solution)/shard_map/all_gather | solution.py:150
  469.2 45.0 %convert_reduce_fusion = (f32[4096]{0:T(1024)}, bf16[864,4096]{1,0:T(8,128)(2,1)S(1)}, f32[864,4096]{1,0:T(8,128)}) fusion(f32[864,4096]{1,0:T(8,128)} %fusion.43, f32[4096]{0:T(1024)S(1)} %copy-done.32, bf16[864,1024]{1,0:T(8,128)(2,1)} %fusion.28, bf16[4096,1024]{1,0:T(8,128)(2,1)} %all-gather.19.cloned.1.call-done), kind=kOutput, calls=%fused_computation.40 | convolution fusion | flops 7513174016 | bytes 45580288 | tf_op jit(solution)/shard_map/dot_general | solution.py:30
  514.2 8.9 multiply_reduce_fusion.1
  532.1 191.2 %while.33 = (s32[]{:T(128)}, bf16[8,4,216,128]{2,3,1,0:T(8,128)(2,1)}, f32[8,4,864,128]{2,3,1,0:T(8,128)}, f32[8,4,864,128]{2,3,1,0:T(8,128)}, s32[8]{0:T(128)S(...) while((s32[]{:T(128)}, ...), condition=%wide.region_12.13_spmd.clone, body=%wide.region_10.12_spmd.clone.sunk | while | flops 978575040 | bytes 83347928 | solution.py:128
  723.3 14.7 copy.43
  738.0 15.7 reshape.276
  753.8 15.2 copy.42
  769.0 16.2 reshape.275
  793.1 15.0 fusion.42
  808.9 11.4 multiply_convert_fusion.1
  823.1 11.6 fusion.52
  842.2 45.3 %reduce-scatter.9.cloned.1.call-done = f32[4,216,1024]{2,1,0:T(8,128)} async-done(((f32[4,864,1024]{2,1,0:T(8,128)}), f32[4,216,1024]{2,1,0:T(8,128)}) %reduce-scatter.9.cloned.1.call-update) | async-done | bytes 3538960 | tf_op jit(solution)/shard_map/reduce_scatter | solution.py:231
  891.0 133.3 %reduce-scatter.7.cloned.1.call-done = f32[4,216,1024]{2,1,0:T(8,128)} async-done(((f32[4,864,1024]{2,1,0:T(8,128)}), f32[4,216,1024]{2,1,0:T(8,128)}) %reduce-scatter.7.cloned.1.call-update) | async-done | bytes 3538960 | tf_op jit(solution)/shard_map/reduce_scatter | solution.py:230
  1028.4 9.8 fusion.40
  1042.7 37.9 %reduce-scatter.13.cloned.1.call-done = f32[256,1024]{1,0:T(8,128)} async-done(((f32[1024,1024]{1,0:T(8,128)}), f32[256,1024]{1,0:T(8,128)}) %reduce-scatter.13.cloned.1.call-update) | async-done | bytes 1048592 | tf_op jit(solution)/shard_map/reduce_scatter | solution.py:261
  1080.6 157.0 %reduce-scatter.15.cloned.1.call-done = f32[256,4096]{1,0:T(8,128)} async-done(((f32[1024,4096]{1,0:T(8,128)}), f32[256,4096]{1,0:T(8,128)}) %reduce-scatter.15.cloned.1.call-update) | async-done | bytes 4194320 | tf_op jit(solution)/shard_map/reduce_scatter | solution.py:262
  1237.6 157.2 %reduce-scatter.17.cloned.1.call-done = f32[1024,1024]{1,0:T(8,128)} async-done(((f32[4096,1024]{1,0:T(8,128)}), f32[1024,1024]{1,0:T(8,128)}) %reduce-scatter.17.cloned.1.call-update) | async-done | bytes 4194320 | tf_op jit(solution)/shard_map/reduce_scatter | solution.py:263
  1394.8 124.0 %reduce-scatter.11.cloned.1.call-done = f32[256,3072]{1,0:T(8,128)} async-done(((f32[1024,3072]{1,0:T(8,128)}), f32[256,3072]{1,0:T(8,128)}) %reduce-scatter.11.cloned.1.call-update) | async-done | bytes 3145744 | tf_op jit(solution)/shard_map/reduce_scatter | solution.py:260
  1519.6 13.1 multiply_convert_fusion.3
  1532.7 12.4 fusion.44
  1558.5 16.8 all-reduce.4
  1577.4 28.9 %all-reduce.2 = (f32[512]{0:T(512)}, f32[2560]{0:T(1024)}) all-reduce(f32[512]{0:T(512)} %dynamic-slice.1, f32[2560]{0:T(1024)S(1)} %dynamic-slice.3), channel_id=1, replica_groups=mesh['replica'=8,'shard'=4] {'replica'}, use_global_device_ids=true, to_apply=%region_28.29 | all-reduce | flops 3072 | bytes 24576 | tf_op jit(solution)/shard_map/psum | solution.py:267
  1612.2 165.8 %all-reduce.7.cloned.1.call-done = (f32[256,3072]{1,0:T(8,128)}, f32[256,1024]{1,0:T(8,128)}, f32[256,4096]{1,0:T(8,128)}, f32[1024,1024]{1,0:T(8,128)}) async-done(((f32[256,3072]{1,0:T(8,128)}, f32[256,1024]{1,0:T(8,128)}, f32[256,4096]{1,0:T(8,128)}, f32[1024,1024]{1,0:T(8,128)}), (f32[256,3072]{1,0:T(8,128)}, f32[256,1024]{1,0:T(8,128)}, f32[256,4096]{1,0:T(8,128)}, ...) | async-done | bytes 12582928 | tf_op jit(solution)/shard_map/psum | solution.py:267
  (508 shorter events, 390.1 us)
Async XLA Ops:
  7.2 13.8 copy-start.5
  7.2 75.6 %all-gather.9.cloned.1.call-start = ((), (), s32[]{:S(2)}) async-start(), calls=%async_computation.6 | async-start | bytes 7864320 | tf_op jit(solution)/shard_map/all_gather | solution.py:147
  7.9 166.2 %all-gather.11.cloned.1.call-start = ((), (), s32[]{:S(2)}) async-start(), calls=%async_computation.7 | async-start | bytes 8847360 | tf_op jit(solution)/shard_map/all_gather | solution.py:173
  9.8 23.7 %copy-start.38 = (f32[864]{0:T(1024)}, f32[864]{0:T(1024)S(1)}, u32[]{:S(2)}) copy-start(f32[864]{0:T(1024)S(1)} %div.53) | copy-start | bytes 10372
  31.0 328.4 %copy-start.34 = (f32[1024]{0:T(1024)}, f32[1024]{0:T(1024)S(1)}, u32[]{:S(2)}) copy-start(f32[1024]{0:T(1024)S(1)} %get-tuple-element.444) | copy-start | bytes 12292
  33.6 57.0 %copy-start.19 = (bf16[864,1024]{1,0:T(8,128)(2,1)}, bf16[864,1024]{1,0:T(8,128)(2,1)S(1)}, u32[]{:S(2)}) copy-start(bf16[864,1024]{1,0:T(8,128)(2,1)S(1)} %get-tuple-element.441) | copy-start | bytes 5308420
  97.2 156.1 %all-gather.13.cloned.1.call-start = ((), (), s32[]{:S(2)}) async-start(), calls=%async_computation.8 | async-start | bytes 8847360 | tf_op jit(solution)/shard_map/all_gather | solution.py:172
  102.2 252.2 %all-gather.15.cloned.1.call-start = ((), (), s32[]{:S(2)}) async-start(), calls=%async_computation.9 | async-start | bytes 2621440 | tf_op jit(solution)/shard_map/all_gather | solution.py:148
  102.7 277.0 %all-gather.17.cloned.1.call-start = ((), (), s32[]{:S(2)}) async-start(), calls=%async_computation.10 | async-start | bytes 10485760 | tf_op jit(solution)/shard_map/all_gather | solution.py:149
  103.3 365.8 %all-gather.19.cloned.1.call-start = ((), (), s32[]{:S(2)}) async-start(), calls=%async_computation.11 | async-start | bytes 10485760 | tf_op jit(solution)/shard_map/all_gather | solution.py:150
  103.9 783.6 %reduce-scatter.9.cloned.1.call-start = ((), (), s32[]{:S(2)}) async-start(), calls=%async_computation.13 | async-start | bytes 17694720 | tf_op jit(solution)/shard_map/reduce_scatter | solution.py:231
  359.0 164.1 %copy-start.2 = (f32[864,1024]{1,0:T(8,128)}, f32[864,1024]{1,0:T(8,128)S(1)}, u32[]{:S(2)}) copy-start(f32[864,1024]{1,0:T(8,128)S(1)} %bitcast_add_fusion) | copy-start | bytes 10616836
  359.4 20.3 %copy-start.48 = (f32[864]{0:T(1024)}, f32[864]{0:T(1024)S(1)}, u32[]{:S(2)}) copy-start(f32[864]{0:T(1024)S(1)} %broadcast_multiply_fusion) | copy-start | bytes 10372
  360.0 19.7 %copy-start.51 = (f32[864]{0:T(1024)}, f32[864]{0:T(1024)S(1)}, u32[]{:S(2)}) copy-start(f32[864]{0:T(1024)S(1)} %multiply_reduce_fusion.5) | copy-start | bytes 10372
  379.7 89.4 %copy-start.32 = (f32[4096]{0:T(1024)S(1)}, f32[4096]{0:T(1024)}, u32[]{:S(2)}) copy-start(f32[4096]{0:T(1024)} %slice.69) | copy-start | bytes 49156
  469.1 45.0 %copy-start.35 = (f32[1024]{0:T(1024)S(1)}, f32[1024]{0:T(1024)}, u32[]{:S(2)}) copy-start(f32[1024]{0:T(1024)} %copy-done.34) | copy-start | bytes 12292
  469.1 45.0 %copy-start.49 = (f32[864]{0:T(1024)S(1)}, f32[864]{0:T(1024)}, u32[]{:S(2)}) copy-start(f32[864]{0:T(1024)} %copy-done.48) | copy-start | bytes 10372
  469.1 45.0 %copy-start.56 = (f32[864]{0:T(1024)S(1)}, f32[864]{0:T(1024)}, u32[]{:S(2)}) copy-start(f32[864]{0:T(1024)} %fusion.39) | copy-start | bytes 10372
  469.1 45.0 %copy-start.58 = (f32[2,1,512]{2,1,0:T(1,128)S(1)}, f32[2,1,512]{2,1,0:T(1,128)}, u32[]{:S(2)}) copy-start(f32[2,1,512]{2,1,0:T(1,128)} %get-tuple-element.448) | copy-start | bytes 12292
  469.2 45.0 %copy-start.65 = (bf16[1024,4096]{1,0:T(8,128)(2,1)S(1)}, bf16[1024,4096]{1,0:T(8,128)(2,1)}, u32[]{:S(2)}) copy-start(bf16[1024,4096]{1,0:T(8,128)(2,1)} %all-gather.17.cloned.1.call-done) | copy-start | bytes 25165828
  753.7 270.6 %reduce-scatter.7.cloned.1.call-start = ((), (), s32[]{:S(2)}) async-start(), calls=%async_computation.12 | async-start | bytes 17694720 | tf_op jit(solution)/shard_map/reduce_scatter | solution.py:230
  785.2 295.4 %reduce-scatter.13.cloned.1.call-start = ((), (), s32[]{:S(2)}) async-start(), calls=%async_computation.15 | async-start | bytes 5242880 | tf_op jit(solution)/shard_map/reduce_scatter | solution.py:261
  791.1 446.5 %reduce-scatter.15.cloned.1.call-start = ((), (), s32[]{:S(2)}) async-start(), calls=%async_computation.16 | async-start | bytes 20971520 | tf_op jit(solution)/shard_map/reduce_scatter | solution.py:262
  808.2 586.6 %reduce-scatter.17.cloned.1.call-start = ((), (), s32[]{:S(2)}) async-start(), calls=%async_computation.17 | async-start | bytes 20971520 | tf_op jit(solution)/shard_map/reduce_scatter | solution.py:263
  808.9 14.2 copy-start.21
  834.7 684.1 %reduce-scatter.11.cloned.1.call-start = ((), (), s32[]{:S(2)}) async-start(), calls=%async_computation.14 | async-start | bytes 15728640 | tf_op jit(solution)/shard_map/reduce_scatter | solution.py:260
  1038.2 739.8 %all-reduce.7.cloned.1.call-start = ((), (), s32[]{:S(2)}) async-start(), calls=%async_computation.18 | async-start | bytes 25165824 | tf_op jit(solution)/shard_map/psum | solution.py:267
  1519.5 13.2 copy-start.6
  1519.5 13.2 copy-start.11
  1519.5 13.2 copy-start.13
  1519.5 13.1 copy-start.15
  1550.7 56.2 %copy-start.1 = (f32[864,1024]{1,0:T(8,128)S(1)}, f32[864,1024]{1,0:T(8,128)}, u32[]{:S(2)}) copy-start(f32[864,1024]{1,0:T(8,128)} %copy-done) | copy-start | bytes 10616836
  (66 other events, 319.5 us)
Sparse Core Ops, SparseCore 0:
  9.9 72.9 all-gather.8
  97.3 76.7 all-gather.10
  176.5 76.6 all-gather.12
  255.0 35.3 all-gather.14
  292.0 87.6 all-gather.16
  381.4 87.6 all-gather.18
  753.8 133.6 reduce-scatter.8
  890.7 133.6 reduce-scatter.6
  1027.8 52.6 reduce-scatter.12
  1083.8 153.7 reduce-scatter.14
  1241.0 153.7 reduce-scatter.16
  1398.1 120.6 reduce-scatter.10
  1521.6 256.3 all-reduce.6
where the time goes:
time: 1810 us; the launch traced here: 1800 us
  waiting for transfers between devices  1100 us (61%)
  matrix products  275 us (15%)
  local copies, waits for them, and re-layouts  256 us (14%)
  other arithmetic  76.5 us (4%)
  blocking collectives  63.4 us (4%)
    psum x1, waiting for transfers between devices, per_device(): lax.psum((group_grads[0], group_grads[1], group_grads[2], group_grads[3],...  166 us
    reduce_scatter x1, waiting for transfers between devices, per_device(): lax.psum_scatter(local_grads[3], 'shard', scatter_dimension=0, tiled=True)  157 us
    reduce_scatter x1, waiting for transfers between devices, per_device(): lax.psum_scatter(local_grads[2], 'shard', scatter_dimension=0, tiled=True)  157 us
    reduce_scatter x1, waiting for transfers between devices, per_device(): lax.psum_scatter(grad_key_all, 'shard', scatter_dimension=1, tiled=True)  133 us
    reduce_scatter x1, waiting for transfers between devices, per_device(): lax.psum_scatter(local_grads[0], 'shard', scatter_dimension=0, tiled=True)  124 us
    all_gather x1, waiting for transfers between devices, per_device(): lax.all_gather(shard_args[3], 'shard', axis=0, tiled=True)  75.5 us
    dot_general x4, matrix products, times_transpose(): lax.dot_general(left, right, (((1,), (1,)), ((), ())), preferred_element_...  69.5 us
    unnamed x157, local copies, waits for them, and re-layouts  66.3 us
  transfers between devices with their start and end apart: 13, of which 12 were waited for; matrix products, arithmetic and copies ran while one was open for 16% of the time, Pallas kernels for 0%

commit v1 on v0

v1 whole, which is shorter than its diff:
```python
import functools

import jax
import jax.numpy as jnp
from jax import lax
from jax.experimental import pallas as pl
from jax.experimental.pallas import tpu as pltpu
from jax.sharding import Mesh, PartitionSpec as P

HEAD = 64
LANES = 2 * HEAD
SCALE = HEAD ** (-0.5)

norm_eps = 1e-06
big_negative = -1e30
BF = jnp.bfloat16
F32 = jnp.float32
SWAP = [(0, 1), (1, 0)]


def layer_norm(values, norm_gain, norm_shift):
    centered = values - jnp.mean(values, axis=-1, keepdims=True)
    spread = jnp.mean(centered * centered, axis=-1, keepdims=True)
    return centered * lax.rsqrt(spread + norm_eps) * norm_gain + norm_shift


def exact_gelu(values):
    return jax.nn.gelu(values, approximate=False)


def rows_inner(left, right):
    return lax.dot_general(left, right, (((0,), (0,)), ((), ())), preferred_element_type=F32)


def times_transpose(left, right):
    return lax.dot_general(left, right, (((1,), (1,)), ((), ())), preferred_element_type=F32)


def times(left, right):
    return jnp.dot(left, right, preferred_element_type=F32)


def softmax_parts(query, mixed_ref, key_masks, sources):
    scores = []
    for b in range(sources):
        key_rows = mixed_ref[b, 0, :, LANES : 2 * LANES]
        scores.append(jnp.where(key_masks[b], times_transpose(query, key_rows) * SCALE, big_negative))
    row_max = functools.reduce(
        jnp.maximum, [jnp.max(part, axis=1, keepdims=True) for part in scores]
    )
    exps = [jnp.exp(part - row_max) for part in scores]
    total = functools.reduce(jnp.add, [jnp.sum(part, axis=1, keepdims=True) for part in exps])
    return exps, 1.0 / total


def masks_of(counts_ref, image, sources, slot):
    column = lax.broadcasted_iota(jnp.int32, (1, slot), 1)
    return [column < counts_ref[image, b] for b in range(sources)]


def forward_kernel(counts_ref, mixed_ref, attended_ref):
    sources, slot = mixed_ref.shape[0], mixed_ref.shape[2]
    key_masks = masks_of(counts_ref, pl.program_id(0), sources, slot)
    low_lanes = lax.broadcasted_iota(jnp.int32, (1, LANES), 1) < HEAD

    def one_source(a, carry):
        query = mixed_ref[a, 0, :, 0:LANES]
        outs = []
        for head in range(2):
            kept = low_lanes if head == 0 else jnp.logical_not(low_lanes)
            own = jnp.where(kept, query, jnp.zeros_like(query))
            exps, inverse = softmax_parts(own, mixed_ref, key_masks, sources)
            out = None
            for b in range(sources):
                probs = (exps[b] * inverse).astype(BF)
                term = times(probs, mixed_ref[b, 0, :, 2 * LANES : 3 * LANES])
                out = term if out is None else out + term
            outs.append(out)
        attended_ref[a, 0] = jnp.where(low_lanes, outs[0], outs[1]).astype(BF)
        return carry

    lax.fori_loop(0, sources, one_source, 0)


def backward_kernel(counts_ref, mixed_ref, grad_ref, out_ref, key_sum, value_sum):
    sources, slot = mixed_ref.shape[0], mixed_ref.shape[2]
    key_masks = masks_of(counts_ref, pl.program_id(0), sources, slot)
    low_lanes = lax.broadcasted_iota(jnp.int32, (1, LANES), 1) < HEAD
    key_sum[...] = jnp.zeros_like(key_sum)
    value_sum[...] = jnp.zeros_like(value_sum)

    def one_source(a, carry):
        query = mixed_ref[a, 0, :, 0:LANES]
        grad = grad_ref[a, 0]
        outs = []
        for head in range(2):
            kept = low_lanes if head == 0 else jnp.logical_not(low_lanes)
            own = jnp.where(kept, query, jnp.zeros_like(query))
            own_grad = jnp.where(kept, grad, jnp.zeros_like(grad))
            exps, inverse = softmax_parts(own, mixed_ref, key_masks, sources)
            probs, grad_probs, inner = [], [], None
            for b in range(sources):
                part = exps[b] * inverse
                grad_part = times_transpose(own_grad, mixed_ref[b, 0, :, 2 * LANES : 3 * LANES])
                term = jnp.sum(part * grad_part, axis=1, keepdims=True)
                inner = term if inner is None else inner + term
                probs.append(part)
                grad_probs.append(grad_part)
                value_sum[b] += rows_inner(part.astype(BF), own_grad)
            out = None
            for b in range(sources):
                grad_scores = (probs[b] * (grad_probs[b] - inner)).astype(BF)
                term = times(grad_scores, mixed_ref[b, 0, :, LANES : 2 * LANES])
                out = term if out is None else out + term
                key_sum[b] += rows_inner(grad_scores, own)
            outs.append(out)
        out_ref[a, 0, :, 0:LANES] = (jnp.where(low_lanes, outs[0], outs[1]) * SCALE).astype(BF)
        return carry

    lax.fori_loop(0, sources, one_source, 0)
    for b in range(sources):
        out_ref[b, 0, :, LANES : 2 * LANES] = (key_sum[b] * SCALE).astype(BF)
        out_ref[b, 0, :, 2 * LANES : 3 * LANES] = value_sum[b].astype(BF)


def attention_specs(sources, slot, width):
    return pl.BlockSpec((sources, 1, slot, width), lambda i, p: (0, i, 0, p))


def attend_forward(counts, mixed):
    sources, images, slot, width = mixed.shape
    pairs = width // (3 * LANES)
    work = 4 * images * pairs * (sources * slot) ** 2 * LANES
    return pl.pallas_call(
        forward_kernel,
        grid=(images, pairs),
        in_specs=[
            pl.BlockSpec(memory_space=pltpu.SMEM),
            attention_specs(sources, slot, 3 * LANES),
        ],
        out_specs=attention_specs(sources, slot, LANES),
        out_shape=jax.ShapeDtypeStruct((sources, images, slot, pairs * LANES), BF),
        compiler_params=pltpu.CompilerParams(vmem_limit_bytes=40 * 2**20),
        cost_estimate=pl.CostEstimate(flops=work, bytes_accessed=mixed.size * 3, transcendentals=0),
    )(counts, mixed)


def attend_backward(counts, mixed, grad_attended):
    sources, images, slot, width = mixed.shape
    pairs = width // (3 * LANES)
    work = 10 * images * pairs * (sources * slot) ** 2 * LANES
    return pl.pallas_call(
        backward_kernel,
        grid=(images, pairs),
        in_specs=[
            pl.BlockSpec(memory_space=pltpu.SMEM),
            attention_specs(sources, slot, 3 * LANES),
            attention_specs(sources, slot, LANES),
        ],
        out_specs=attention_specs(sources, slot, 3 * LANES),
        out_shape=jax.ShapeDtypeStruct(mixed.shape, BF),
        scratch_shapes=[
            pltpu.VMEM((sources, slot, LANES), F32),
            pltpu.VMEM((sources, slot, LANES), F32),
        ],
        compiler_params=pltpu.CompilerParams(vmem_limit_bytes=40 * 2**20),
        cost_estimate=pl.CostEstimate(flops=work, bytes_accessed=mixed.size * 5, transcendentals=0),
    )(counts, mixed, grad_attended)


def reduce_weight(grad, shards):
    rows, columns = grad.shape
    core = lax.axis_index("core")
    halves = grad.reshape(shards, 2, rows // shards // 2, columns)
    own = lax.dynamic_index_in_dim(halves, core, 1, keepdims=False)
    other = lax.dynamic_index_in_dim(halves, 1 - core, 1, keepdims=False).astype(BF)
    received = lax.ppermute(other, "core", SWAP)
    chip = (own + received.astype(F32)).astype(BF).reshape(rows // 2, columns)
    group = lax.psum_scatter(chip, "shard", scatter_dimension=0, tiled=True)
    total = lax.psum(group, "rep")
    partner = lax.ppermute(total, "core", SWAP)
    pair = jnp.stack([jnp.where(core == 0, total, partner), jnp.where(core == 0, partner, total)])
    return pair.reshape(rows // shards, columns).astype(F32)


def per_device(tokens, counts, w_qkv, w_proj, w_fc1, w_fc2, norm_gains, biases, grad_out):
    images, slot_rows, width = tokens.shape
    shards = lax.axis_size("shard")
    shard_rank = lax.axis_index("shard")
    row_count = images * slot_rows
    shaped = (images, slot_rows, width)
    pairs = width // LANES
    own_counts = lax.dynamic_slice_in_dim(counts, shard_rank, 1, 1)
    slot_index = jnp.arange(slot_rows, dtype=jnp.int32)
    row_valid = (slot_index[None, :] < own_counts).astype(F32).reshape(row_count, 1)

    qkv_paired = w_qkv.reshape(-1, 3, pairs, LANES).swapaxes(1, 2).reshape(w_qkv.shape)
    vectors = lax.all_gather(jnp.concatenate([norm_gains, biases]), "shard", axis=0, tiled=False)
    gain_len = norm_gains.shape[0]
    gains_wide = vectors[:, :gain_len].reshape(-1).astype(F32)
    biases_wide = vectors[:, gain_len:].reshape(-1).astype(F32)
    qkv_full = lax.all_gather(qkv_paired, "shard", axis=0, tiled=True)
    proj_full = lax.all_gather(w_proj, "shard", axis=0, tiled=True)
    fc1_full = lax.all_gather(w_fc1, "shard", axis=0, tiled=True)
    fc2_full = lax.all_gather(w_fc2, "shard", axis=0, tiled=True)

    inputs = tokens.astype(F32).reshape(row_count, width)
    normed_wide, norm_one_back = jax.vjp(
        layer_norm, inputs, gains_wide[:width], biases_wide[:width]
    )
    normed_one = normed_wide.astype(BF)
    query_bias = biases_wide[2 * width : 3 * width].reshape(pairs, 1, LANES)
    value_bias = biases_wide[3 * width : 4 * width].reshape(pairs, 1, LANES)
    mixed_bias = jnp.concatenate([query_bias, jnp.zeros_like(query_bias), value_bias], axis=1)
    mixed = (times(normed_one, qkv_full) + mixed_bias.reshape(1, 3 * width)).astype(BF)
    own_heads = lax.all_to_all(
        mixed.reshape(row_count, shards, -1), "shard", split_axis=1, concat_axis=0
    )
    own_heads = own_heads.reshape(shards, images, slot_rows, -1)
    attended = attend_forward(counts, own_heads)
    attended = lax.all_to_all(
        attended.reshape(shards, row_count, -1), "shard", split_axis=0, concat_axis=1
    ).reshape(row_count, width)
    middle = inputs + times(attended, proj_full) + biases_wide[4 * width : 5 * width]
    normed_mid, norm_two_back = jax.vjp(
        layer_norm, middle, gains_wide[width:], biases_wide[width : 2 * width]
    )
    normed_two = normed_mid.astype(BF)
    before = times(normed_two, fc1_full) + biases_wide[6 * width :]
    hidden_wide, gelu_back = jax.vjp(exact_gelu, before)
    hidden = hidden_wide.astype(BF)
    outcome = (middle + times(hidden, fc2_full) + biases_wide[5 * width : 6 * width]) * row_valid
    output = outcome.astype(BF).reshape(shaped)

    grad_rows = grad_out.astype(F32).reshape(row_count, width) * row_valid
    grad_branch = grad_rows.astype(BF)
    grad_fc2 = reduce_weight(rows_inner(hidden, grad_branch), shards)
    grad_out_bias = jnp.sum(grad_branch, axis=0, dtype=F32)
    grad_hidden = times_transpose(grad_branch, fc2_full)
    grad_before = gelu_back(grad_hidden)[0].astype(BF)
    grad_fc1 = reduce_weight(rows_inner(normed_two, grad_before), shards)
    grad_hidden_bias = jnp.sum(grad_before, axis=0, dtype=F32)
    grad_normed_two = times_transpose(grad_before, fc1_full)
    grad_middle_norm, grad_gain_two, grad_shift_two = norm_two_back(grad_normed_two)
    grad_middle = grad_rows + grad_middle_norm
    grad_branch_one = grad_middle.astype(BF)
    grad_proj = reduce_weight(rows_inner(attended, grad_branch_one), shards)
    grad_proj_bias = jnp.sum(grad_branch_one, axis=0, dtype=F32)
    grad_attended = times_transpose(grad_branch_one, proj_full).astype(BF)
    grad_heads = lax.all_to_all(
        grad_attended.reshape(row_count, shards, -1), "shard", split_axis=1, concat_axis=0
    ).reshape(shards, images, slot_rows, -1)
    grad_own = attend_backward(counts, own_heads, grad_heads)
    grad_mixed = lax.all_to_all(
        grad_own.reshape(shards, row_count, -1), "shard", split_axis=0, concat_axis=1
    ).reshape(row_count, 3 * width)
    grad_qkv = reduce_weight(rows_inner(normed_one, grad_mixed), shards)
    grad_qkv = grad_qkv.reshape(-1, pairs, 3, LANES).swapaxes(1, 2).reshape(w_qkv.shape)
    column_sums = jnp.sum(grad_mixed, axis=0, dtype=F32).reshape(pairs, 3, LANES)
    grad_normed_one = times_transpose(grad_mixed, qkv_full)
    grad_inputs_norm, grad_gain_one, grad_shift_one = norm_one_back(grad_normed_one)
    grad_tokens = (grad_middle + grad_inputs_norm).reshape(shaped)
    grad_gains = jnp.concatenate([grad_gain_one, grad_gain_two]).reshape(shards, -1)
    grad_biases = jnp.concatenate(
        [
            grad_shift_one,
            grad_shift_two,
            column_sums[:, 0].reshape(-1),
            column_sums[:, 2].reshape(-1),
            grad_proj_bias,
            grad_out_bias,
            grad_hidden_bias,
        ]
    ).reshape(shards, -1)
    grad_vectors = lax.psum(
        jnp.concatenate([grad_gains, grad_biases], axis=1), ("rep", "core", "shard")
    )
    own_vectors = lax.dynamic_index_in_dim(grad_vectors, shard_rank, 0, keepdims=False)
    return (
        output,
        grad_tokens,
        grad_qkv,
        grad_proj,
        grad_fc1,
        grad_fc2,
        own_vectors[:gain_len],
        own_vectors[gain_len:],
    )


def solution(mesh):
    replicas, shards = mesh.devices.shape
    split = Mesh(mesh.devices.reshape(replicas // 2, 2, shards), ("rep", "core", "shard"))
    both = ("rep", "core")
    rows, weight, vector = P(both, "shard", None), P("shard", None), P("shard")
    in_specs = (rows, P(both, None)) + (weight,) * 4 + (vector,) * 2 + (rows,)
    out_specs = (rows, rows) + (weight,) * 4 + (vector,) * 2
    return jax.shard_map(
        per_device, mesh=split, in_specs=in_specs, out_specs=out_specs, check_vma=False
    )
```

time: 1810 us -> 974 us (0.54)
  waiting for transfers between devices: 1100 us -> 257 us
  local copies, waits for them, and re-layouts: 256 us -> 122 us
  Pallas kernels: 0 us -> 125 us
  blocking collectives: 63.4 us -> 186 us
  matrix products: 275 us -> 186 us
    reduce_scatter x6 -> x4, waiting for transfers between devices: 655 us -> 20.3 us  [reduce_weight(): group = lax.psum_scatter(chip, 'shard', scatter_dimension=0, tiled=True)]
    all_gather x6 -> x4, waiting for transfers between devices: 273 us -> 55.9 us  [the longest x1 55.9 us: per_device(): qkv_full = lax.all_gather(qkv_paired, 'shard', axis=0, tiled=True)]
    all_to_all x0 -> x2, blocking collectives: none -> 137 us  [the longest x1 92.9 us: per_device(): lax.all_to_all(mixed.reshape(row_count, shards, -1), 'shard', split_axis=...]
    pallas_call x0 -> x2, Pallas kernels: none -> 125 us  [the longest x1 81.6 us: attend_backward(): pl.pallas_call(backward_kernel, grid=(images, pairs), in_specs=[pl.BlockS...]
    dot_general x60 -> x4, matrix products: 165 us -> 77.4 us  [times(): return jnp.dot(left, right, preferred_element_type=F32)]
    all_to_all x0 -> x2, waiting for transfers between devices: none -> 85.3 us  [the longest x1 69.7 us: per_device(): lax.all_to_all(grad_own.reshape(shards, row_count, -1), 'shard', split_ax...]
    psum x1, waiting for transfers between devices: 166 us -> 85.1 us  [reduce_weight(): total = lax.psum(group, 'rep')]
    dynamic_slice x72 -> x0, local copies, waits for them, and re-layouts: 67.6 us -> none  [the longest x56 58.3 us: pair_slice(): piece = lax.dynamic_slice_in_dim(source, column_start, 2 * HEAD, 2)]
  transfers between devices with their start and end apart: 13 -> 19, of which waited for: 12 -> 7; matrix products, arithmetic and copies ran while one was open for 16% -> 35% of each run, Pallas kernels for 0% -> 13%
where the time goes in v1:
time: 974 us; the launch traced here: 966 us
  waiting for transfers between devices  257 us (26%)
  blocking collectives  186 us (19%)
  matrix products  186 us (19%)
  Pallas kernels  125 us (13%)
  local copies, waits for them, and re-layouts  122 us (13%)
  other arithmetic  62.6 us (6%)
  between operations  14.9 us (2%)
  starting transfers between devices  12 us (1%)
    all_to_all x1, blocking collectives, per_device(): lax.all_to_all(mixed.reshape(row_count, shards, -1), 'shard', split_axis=...  92.9 us
    psum x1, waiting for transfers between devices, reduce_weight(): total = lax.psum(group, 'rep')  85.1 us
    pallas_call x1, Pallas kernels, attend_backward(): pl.pallas_call(backward_kernel, grid=(images, pairs), in_specs=[pl.BlockS...  81.6 us
    dot_general x4, matrix products, times(): return jnp.dot(left, right, preferred_element_type=F32)  77.4 us
    dot_general x4, matrix products, times_transpose(): lax.dot_general(left, right, (((1,), (1,)), ((), ())), preferred_element_...  73.5 us
    all_to_all x1, waiting for transfers between devices, per_device(): lax.all_to_all(grad_own.reshape(shards, row_count, -1), 'shard', split_ax...  69.7 us
    all_gather x1, waiting for transfers between devices, per_device(): qkv_full = lax.all_gather(qkv_paired, 'shard', axis=0, tiled=True)  55.9 us
    all_to_all x1, blocking collectives, per_device(): lax.all_to_all(grad_attended.reshape(row_count, shards, -1), 'shard', spl...  43.8 us
  transfers between devices with their start and end apart: 19, of which 7 were waited for; matrix products, arithmetic and copies ran while one was open for 35% of the time, Pallas kernels for 13%

profile of v1, /device:TPU:0, one launch (start us, length us, event | category | flops | bytes accessed | tf_op | source)
XLA Modules:
  0.0 966.3 jit_solution(14481512424619800198)
XLA Ops:
  11.9 9.6 all-gather
  27.3 55.9 %all-gather.6.cloned.1.call-done = bf16[1024,3072]{0,1:T(8,128)(2,1)} async-done(((bf16[256,3072]{0,1:T(8,128)(2,1)}), bf16[1024,3072]{0,1:T(8,128)(2,1)}) %all-gather.6.cloned.1.call-update) | async-done | bytes 6291472 | tf_op jit(solution)/shard_map/all_gather | solution.py:202
  83.2 10.2 %add_convert_fusion.1 = bf16[864,3072]{1,0:T(8,128)(2,1)} fusion(bf16[864,1024]{1,0:T(8,128)(2,1)S(1)} %get-tuple-element.48, bf16[1024,3072]{0,1:T(8,128)(2,1)} %all-gather.6.cloned.1.call-done, f32[3072]{0:T(1024)} %add.143), kind=kOutput, calls=%fused_computation.42 | convolution fusion | flops 5441126400 | bytes 13381632 | tf_op jit(solution)/shard_map/dot_general | solution.py:40
  93.4 10.6 %broadcast_in_dim_reshape.12 = bf16[1,864,4,768]{3,2,1,0:T(4,128)(2,1)} reshape(bf16[864,3072]{1,0:T(8,128)(2,1)} %add_convert_fusion.1) | data formatting | bytes 10616832 | tf_op jit(solution)/shard_map/broadcast_in_dim;reshape | solution.py:216
  107.2 92.9 %all_to_all.60 = bf16[1,864,4,768]{3,1,0,2:T(8,128)(2,1)S(1)} all-to-all(bf16[1,864,4,768]{3,1,0,2:T(8,128)(2,1)S(1)} %copy.46), channel_id=1, replica_groups=mesh['rep'=4,'core'=2,'shard'=4] {'shard'}, dimensions={2} | all-to-all | bytes 10616832 | tf_op jit(solution)/shard_map/all_to_all | solution.py:216
  200.2 43.5 %shard_map.152 = bf16[4,4,216,256]{3,2,1,0:T(8,128)(2,1)} custom-call(s32[4,4]{1,0:T(4,128)S(1)} %copy-done.3, bf16[4,4,216,768]{3,2,1,0:T(8,128)(2,1)S(1)} %bitcast.222), custom_call_target="tpu_custom_call" | custom-call | flops 3057647616 | bytes 7962624 | tf_op jit(solution)/shard_map/pallas_call | solution.py:134
  255.2 15.6 %all-to-all-done.1 = bf16[4,864,1,256]{3,1,2,0:T(8,128)(2,1)S(1)} async-done(((bf16[4,864,1,256]{3,1,2,0:T(8,128)(2,1)}), bf16[4,864,1,256]{3,1,2,0:T(8,128)(2,1)S(1)}, u32[]{:S(2)}, u32[]{:S(2)}) %all-to-all-start.1) | async-done | bytes 1769504 | tf_op jit(solution)/shard_map/all_to_all | solution.py:221
  273.1 5.4 bitcast_add_fusion.3
  280.9 42.5 %fusion.3 = (bf16[4096,864]{0,1:T(8,128)(2,1)}, f32[864,4096]{1,0:T(8,128)}) fusion(f32[4096]{0:T(1024)} %slice.87, bf16[1024,4096]{1,0:T(8,128)(2,1)} %all-gather.10.cloned.1.call-done, f32[864,1024]{1,0:T(8,128)S(1)} %bitcast_add_fusion.3, f32[1024]{0:T(1024)} %get-tuple-element.53, f32[1024]{0:T(1024)S(1)} %bitcast.250, f32[864]{0:T(1024)} %fusion.46, ...), kind=kOutput, calls=%fused_computation.5 | convolution fusion | flops 7486636032 | bytes 33196800 | tf_op jit(solution)/shard_map/dot_general | solution.py:40
  323.4 16.9 %dot_general.61 = bf16[4,2,512,864]{2,1,0,3:T(2,128)(2,1)} reshape(bf16[4096,864]{0,1:T(8,128)(2,1)} %get-tuple-element.65) | data formatting | bytes 14155776 | tf_op jit(solution)/shard_map/dot_general | solution.py:32
  340.2 11.8 %fusion.26 = f32[4,2,512,1024]{3,2,1,0:T(8,128)S(1)} fusion(bf16[864,1024,1,1]{1,0,3,2:T(8,128)(2,1)S(1)} %bitcast.245, bf16[4,2,512,864]{2,1,0,3:T(2,128)(2,1)} %dot_general.61), kind=kOutput, calls=%fused_computation.50 | convolution fusion | flops 7247757312 | bytes 25624576 | tf_op jit(solution)/shard_map/dot_general | solution.py:32
  352.1 5.7 copy-done.11
  360.6 44.7 %convert_reduce_fusion = (f32[4096]{0:T(1024)}, bf16[864,4096]{1,0:T(8,128)(2,1)S(1)}, f32[864,4096]{1,0:T(8,128)}) fusion(f32[864,4096]{1,0:T(8,128)} %get-tuple-element.66, f32[4096]{0:T(1024)} %slice.87, bf16[864,1024]{1,0:T(8,128)(2,1)} %fusion.37, bf16[4096,1024]{1,0:T(8,128)(2,1)} %all-gather.12.cloned.1.call-done), kind=kOutput, calls=%fused_computation.11 | convolution fusion | flops 7513174016 | bytes 45580288 | tf_op jit(solution)/shard_map/dot_general | solution.py:36
  405.3 13.9 %multiply_reduce_fusion = (f32[1024]{0:T(1024)}, f32[864]{0:T(1024)S(1)}, f32[1024]{0:T(1024)}, f32[864,1024]{1,0:T(8,128)S(1)}) fusion(f32[864,1024]{1,0:T(8,128)S(1)} %copy-done.7, f32[864]{0:T(1024)S(1)} %copy-done.42, f32[864]{0:T(1024)S(1)} %copy-done.37, f32[1024]{0:T(1024)S(1)} %copy-done.26, f32[1024]{0:T(1024)S(1)} %bitcast.251, ...), kind=kOutput, calls=%fused_computation.72 | convolution fusion | flops 7255716864 | bytes 22571136 | tf_op jit(solution)/shard_map/dot_general | solution.py:36
  434.6 8.3 fusion.23
  443.0 12.4 %fusion.49 = f32[1024,4096]{1,0:T(8,128)S(1)} fusion(bf16[864,4096]{1,0:T(8,128)(2,1)} %copy-done.51, f32[864,1024]{1,0:T(8,128)S(1)} %copy-done.7, f32[1024]{0:T(1024)} %get-tuple-element.53, f32[1024]{0:T(1024)} %bitcast.249, f32[864]{0:T(1024)} %fusion.46, f32[864]{0:T(1024)S(1)} %copy-done.37, f32[1024]{0:T(1024)S(1)} %copy-done.26), kind=kOutput, calls=%fused_computation.141 | convolution fusion | flops 7253065728 | bytes 27413248 | tf_op jit(solution)/shard_map/dot_general | solution.py:32
  455.4 7.1 copy-done.12
  469.2 43.8 %all_to_all.61 = bf16[1,864,4,256]{3,1,0,2:T(8,128)(2,1)S(1)} all-to-all(bf16[1,864,4,256]{3,1,0,2:T(8,128)(2,1)S(1)} %copy.49), channel_id=1, replica_groups=mesh['rep'=4,'core'=2,'shard'=4] {'shard'}, dimensions={2} | all-to-all | bytes 3538944 | tf_op jit(solution)/shard_map/all_to_all | solution.py:250
  515.6 81.6 %shard_map.153 = bf16[4,4,216,768]{3,2,1,0:T(8,128)(2,1)S(1)} custom-call(s32[4,4]{1,0:T(4,128)S(1)} %copy-done.3, bf16[4,4,216,768]{3,2,1,0:T(8,128)(2,1)S(1)} %bitcast.223, bf16[4,4,216,256]{3,2,1,0:T(8,128)(2,1)S(1)} %bitcast.225), custom_call_target="tpu_custom_call" | custom-call | flops 7644119040 | bytes 13271040 | tf_op jit(solution)/shard_map/pallas_call | solution.py:152
  605.0 8.1 fusion.24
  615.8 69.7 %all-to-all-done.3 = bf16[4,864,1,768]{3,1,2,0:T(8,128)(2,1)} async-done(((bf16[4,864,1,768]{3,1,2,0:T(8,128)(2,1)}), bf16[4,864,1,768]{3,1,2,0:T(8,128)(2,1)}, u32[]{:S(2)}, u32[]{:S(2)}) %all-to-all-start.3) | async-done | bytes 5308448 | tf_op jit(solution)/shard_map/all_to_all | solution.py:254
  685.5 9.0 copy.51
  694.5 10.1 %reshape.268 = bf16[864,3072,1,1]{1,0,2,3:T(8,128)(2,1)} reshape(bf16[1,864,4,1,768]{4,2,1,3,0:T(4,128)(2,1)} %copy.51) | data formatting | bytes 10616832 | tf_op jit(solution)/shard_map/reshape;squeeze | solution.py:256
  704.6 8.7 fusion.31
  713.9 5.6 collective-permute-done
  723.1 19.3 %multiply_convert_fusion.3 = bf16[864,1024]{1,0:T(8,128)(2,1)} fusion(f32[864,1024]{1,0:T(8,128)} %copy-done.6, f32[864]{0:T(1024)S(1)} %copy-done.24, f32[1024]{0:T(1024)S(1)} %copy-done.48, f32[1024]{0:T(1024)S(1)} %copy-done.26, bf16[4096,1024]{1,0:T(8,128)(2,1)} %all-gather.12.cloned.1.call-done, f32[864,4096]{1,0:T(8,128)} %get-tuple-element.36, ...), kind=kOutput, calls=%fused_computation.79 | convolution fusion | flops 7266336768 | bytes 42036608 | tf_op jit(solution)/shard_map/dot_general | solution.py:40
  746.1 20.3 %reduce-scatter.5.cloned.1.call-done = bf16[128,3072]{1,0:T(8,128)(2,1)} async-done(((bf16[512,3072]{1,0:T(8,128)(2,1)}), bf16[128,3072]{1,0:T(8,128)(2,1)}) %reduce-scatter.5.cloned.1.call-update) | async-done | bytes 786448 | tf_op jit(solution)/shard_map/reduce_scatter | solution.py:179
  766.5 12.7 %multiply_reduce_fusion.1 = (f32[1024]{0:T(1024)S(1)}, f32[864]{0:T(1024)S(1)}, f32[1024]{0:T(1024)}, f32[864,1024]{1,0:T(8,128)}) fusion(f32[864]{0:T(1024)S(1)} %copy-done.30, f32[864]{0:T(1024)S(1)} %copy-done.28, bf16[4,216,1024]{2,1,0:T(8,128)(2,1)} %param.9, f32[864,1024]{1,0:T(8,128)} %get-tuple-element.47, f32[1024]{0:T(1024)S(1)} %bitcast.247, ...), kind=kOutput, calls=%fused_computation.73 | convolution fusion | flops 5443777536 | bytes 20469888 | tf_op jit(solution)/shard_map/dot_general | solution.py:36
  783.7 5.4 add_add_fusion
  801.2 5.1 add_add_fusion.2
  806.3 85.1 %all-reduce.3.cloned.1.call-done = (bf16[128,3072]{1,0:T(8,128)(2,1)}, bf16[128,1024]{1,0:T(8,128)(2,1)}, bf16[128,4096]{1,0:T(8,128)(2,1)}, bf16[512,1024]{1,0:T(8,128)(2,1)}) async-done(((bf16[128,3072]{1,0:T(8,128)(2,1)}, bf16[128,1024]{1,0:T(8,128)(2,1)}, bf16[128,4096]{1,0:T(8,128)(2,1)}, bf16[512,1024]{1,0:T(8,128)(2,1)}), (bf16[128,3072]{1,0:T(8,128)(2,1)}, bf16[128,1024]{1,0:T(8,128)(2,1)}, ...) | async-done | bytes 3145744 | tf_op jit(solution)/shard_map/psum | solution.py:180
  892.7 39.8 %psum.39 = f32[4,3072]{1,0:T(4,128)S(1)} all-reduce(f32[4,3072]{1,0:T(4,128)S(1)} %pad_maximum_fusion.3), channel_id=1, replica_groups=mesh['rep'=4,'core'=2,'shard'=4] {'rep','core','shard'}, use_global_device_ids=true, to_apply=%region_24.25 | all-reduce | flops 12288 | bytes 98304 | tf_op jit(solution)/shard_map/psum | solution.py:275
  (234 shorter events, 119.8 us)
Async XLA Ops:
  7.2 76.0 %all-gather.6.cloned.1.call-start = ((), (), s32[]{:S(2)}) async-start(), calls=%async_computation.8 | async-start | bytes 7864320 | tf_op jit(solution)/shard_map/all_gather | solution.py:202
  10.4 262.7 %all-gather.8.cloned.1.call-start = ((), (), s32[]{:S(2)}) async-start(), calls=%async_computation.9 | async-start | bytes 2621440 | tf_op jit(solution)/shard_map/all_gather | solution.py:203
  11.1 269.8 %all-gather.10.cloned.1.call-start = ((), (), s32[]{:S(2)}) async-start(), calls=%async_computation.10 | async-start | bytes 10485760 | tf_op jit(solution)/shard_map/all_gather | solution.py:204
  22.0 71.4 %copy-start.27 = (f32[864]{0:T(1024)}, f32[864]{0:T(1024)S(1)}, u32[]{:S(2)}) copy-start(f32[864]{0:T(1024)S(1)} %div.39) | copy-start | bytes 10372
  22.8 70.6 %copy-start.29 = (f32[864]{0:T(1024)}, f32[864]{0:T(1024)S(1)}, u32[]{:S(2)}) copy-start(f32[864]{0:T(1024)S(1)} %rsqrt.20) | copy-start | bytes 10372
  23.4 70.0 %copy-start.31 = (f32[1,4,2,128]{3,1,2,0:T(4,128)}, f32[1,4,2,128]{3,1,2,0:T(4,128)S(1)}, u32[]{:S(2)}) copy-start(f32[1,4,2,128]{3,1,2,0:T(4,128)S(1)} %copy.62) | copy-start | bytes 12292
  24.8 256.1 %copy-start.25 = (f32[1024]{0:T(1024)}, f32[1024]{0:T(1024)S(1)}, u32[]{:S(2)}) copy-start(f32[1024]{0:T(1024)S(1)} %get-tuple-element.55) | copy-start | bytes 12292
  27.3 66.1 %copy-start.13 = (bf16[864,1024]{1,0:T(8,128)(2,1)}, bf16[864,1024]{1,0:T(8,128)(2,1)S(1)}, u32[]{:S(2)}) copy-start(bf16[864,1024]{1,0:T(8,128)(2,1)S(1)} %get-tuple-element.48) | copy-start | bytes 5308420
  107.2 92.9 %copy-start.3 = (s32[4,4]{1,0:T(4,128)S(1)}, s32[4,4]{1,0:T(4,128)}, u32[]{:S(2)}) copy-start(s32[4,4]{1,0:T(4,128)} %counts_ref.3) | copy-start | bytes 196
  243.6 27.2 %all-to-all-start.1 = ((bf16[4,864,1,256]{3,1,2,0:T(8,128)(2,1)}), bf16[4,864,1,256]{3,1,2,0:T(8,128)(2,1)S(1)}, u32[]{:S(2)}, u32[]{:S(2)}) async-start(bf16[4,864,1,256]{3,1,2,0:T(8,128)(2,1)} %bitcast.8), calls=%async_computation.1 | async-start | bytes 3538944 | tf_op jit(solution)/shard_map/all_to_all | solution.py:221
  247.4 113.1 %all-gather.12.cloned.1.call-start = ((), (), s32[]{:S(2)}) async-start(), calls=%async_computation.11 | async-start | bytes 10485760 | tf_op jit(solution)/shard_map/all_gather | solution.py:205
  247.9 498.2 %reduce-scatter.7.cloned.1.call-start = ((), (), s32[]{:S(2)}) async-start(), calls=%async_computation.13 | async-start | bytes 1310720 | tf_op jit(solution)/shard_map/reduce_scatter | solution.py:179
  278.5 44.8 %copy-start.6 = (f32[864,1024]{1,0:T(8,128)}, f32[864,1024]{1,0:T(8,128)S(1)}, u32[]{:S(2)}) copy-start(f32[864,1024]{1,0:T(8,128)S(1)} %bitcast_add_fusion.3) | copy-start | bytes 10616836
  360.5 74.1 %collective-permute-start.6 = (bf16[4,512,1024]{2,1,0:T(8,128)(2,1)}, bf16[4,512,1024]{2,1,0:T(8,128)(2,1)}, u32[]{:S(2)}, u32[]{:S(2)}) collective-permute-start(bf16[4,512,1024]{2,1,0:T(8,128)(2,1)} %fusion.34), channel_id=1, source_target_pairs={{0,4},{4,0},{1,5},{5,1},{2,6},{6,2},{3,7},{7,3},{8,12},{12,8},{9,1... | collective-permute-start | bytes 12582920 | tf_op jit(solution)/shard_map/ppermute | solution.py:177
  360.5 44.8 %copy-start.7 = (f32[864,1024]{1,0:T(8,128)S(1)}, f32[864,1024]{1,0:T(8,128)}, u32[]{:S(2)}) copy-start(f32[864,1024]{1,0:T(8,128)} %copy-done.6) | copy-start | bytes 10616836
  360.5 44.8 %copy-start.26 = (f32[1024]{0:T(1024)S(1)}, f32[1024]{0:T(1024)}, u32[]{:S(2)}) copy-start(f32[1024]{0:T(1024)} %copy-done.25) | copy-start | bytes 12292
  360.5 44.8 %copy-start.37 = (f32[864]{0:T(1024)S(1)}, f32[864]{0:T(1024)}, u32[]{:S(2)}) copy-start(f32[864]{0:T(1024)} %copy-done.36) | copy-start | bytes 10372
  360.5 44.8 %copy-start.41 = (f32[1,4,2,128]{3,1,2,0:T(4,128)S(1)}, f32[1,4,2,128]{3,1,2,0:T(4,128)}, u32[]{:S(2)}) copy-start(f32[1,4,2,128]{3,1,2,0:T(4,128)} %copy.63) | copy-start | bytes 12292
  428.2 3.1 collective-permute-start.2
  434.6 311.5 %reduce-scatter.11.cloned.1.call-start = ((), (), s32[]{:S(2)}) async-start(), calls=%async_computation.15 | async-start | bytes 5242880 | tf_op jit(solution)/shard_map/reduce_scatter | solution.py:179
  465.1 139.8 %collective-permute-start.4 = (bf16[4,128,4096]{2,1,0:T(8,128)(2,1)}, bf16[4,128,4096]{2,1,0:T(8,128)(2,1)}, u32[]{:S(2)}, u32[]{:S(2)}) collective-permute-start(bf16[4,128,4096]{2,1,0:T(8,128)(2,1)} %fusion.33), channel_id=1, source_target_pairs={{0,4},{4,0},{1,5},{5,1},{2,6},{6,2},{3,7},{7,3},{8,12},{12,8},{9,1... | collective-permute-start | bytes 12582920 | tf_op jit(solution)/shard_map/ppermute | solution.py:177
  599.7 85.8 %all-to-all-start.3 = ((bf16[4,864,1,768]{3,1,2,0:T(8,128)(2,1)}), bf16[4,864,1,768]{3,1,2,0:T(8,128)(2,1)}, u32[]{:S(2)}, u32[]{:S(2)}) async-start(bf16[4,864,1,768]{3,1,2,0:T(8,128)(2,1)} %bitcast.224), calls=%async_computation.3 | async-start | bytes 10616832 | tf_op jit(solution)/shard_map/all_to_all | solution.py:254
  604.7 141.4 %reduce-scatter.9.cloned.1.call-start = ((), (), s32[]{:S(2)}) async-start(), calls=%async_computation.14 | async-start | bytes 5242880 | tf_op jit(solution)/shard_map/reduce_scatter | solution.py:179
  613.1 153.4 %reduce-scatter.5.cloned.1.call-start = ((), (), s32[]{:S(2)}) async-start(), calls=%async_computation.12 | async-start | bytes 3932160 | tf_op jit(solution)/shard_map/reduce_scatter | solution.py:179
  713.8 5.7 collective-permute-start
  722.3 169.1 %all-reduce.3.cloned.1.call-start = ((), (), s32[]{:S(2)}) async-start(), calls=%async_computation.16 | async-start | bytes 6291456 | tf_op jit(solution)/shard_map/psum | solution.py:180
  801.2 90.7 %copy-start.43 = (f32[2,512]{1,0:T(2,128)S(1)}, f32[2,512]{1,0:T(2,128)}, u32[]{:S(2)}) copy-start(f32[2,512]{1,0:T(2,128)} %concatenate.23) | copy-start | bytes 12292
  801.2 90.7 %copy-start.44 = (f32[2,512]{1,0:T(2,128)S(1)}, f32[2,512]{1,0:T(2,128)}, u32[]{:S(2)}) copy-start(f32[2,512]{1,0:T(2,128)} %concatenate.22) | copy-start | bytes 12292
  891.4 43.0 %collective-permute-start.3 = (bf16[128,1024]{1,0:T(8,128)(2,1)}, bf16[128,1024]{1,0:T(8,128)(2,1)S(1)}, u32[]{:S(2)}, u32[]{:S(2)}) collective-permute-start(bf16[128,1024]{1,0:T(8,128)(2,1)} %get-tuple-element.31), channel_id=1, source_target_pairs={{0,4},{4,0},{1,5},{5,1},{2,6},{6,2},{3,7},{7,3},{8,12},{12,8},{9,1... | collective-permute-start | bytes 786440 | tf_op jit(solution)/shard_map/ppermute | solution.py:181
  891.4 45.1 %collective-permute-start.1 = (bf16[128,3072]{1,0:T(8,128)(2,1)}, bf16[128,3072]{1,0:T(8,128)(2,1)S(1)}, u32[]{:S(2)}, u32[]{:S(2)}) collective-permute-start(bf16[128,3072]{1,0:T(8,128)(2,1)} %get-tuple-element.30), channel_id=1, source_target_pairs={{0,4},{4,0},{1,5},{5,1},{2,6},{6,2},{3,7},{7,3},{8,12},{12,8},{9,1... | collective-permute-start | bytes 2359304 | tf_op jit(solution)/shard_map/ppermute | solution.py:181
  933.8 21.4 %collective-permute-start.5 = (bf16[128,4096]{1,0:T(8,128)(2,1)}, bf16[128,4096]{1,0:T(8,128)(2,1)}, u32[]{:S(2)}, u32[]{:S(2)}) collective-permute-start(bf16[128,4096]{1,0:T(8,128)(2,1)} %get-tuple-element.32), channel_id=1, source_target_pairs={{0,4},{4,0},{1,5},{5,1},{2,6},{6,2},{3,7},{7,3},{8,12},{12,8},{9,1... | collective-permute-start | bytes 3145736 | tf_op jit(solution)/shard_map/ppermute | solution.py:181
  933.8 17.2 %collective-permute-start.7 = (bf16[512,1024]{1,0:T(8,128)(2,1)}, bf16[512,1024]{1,0:T(8,128)(2,1)}, u32[]{:S(2)}, u32[]{:S(2)}) collective-permute-start(bf16[512,1024]{1,0:T(8,128)(2,1)} %get-tuple-element.33), channel_id=1, source_target_pairs={{0,4},{4,0},{1,5},{5,1},{2,6},{6,2},{3,7},{7,3},{8,12},{12,8},{9,1... | collective-permute-start | bytes 3145736 | tf_op jit(solution)/shard_map/ppermute | solution.py:181
  (41 other events, 468.6 us)
Sparse Core Ops, SparseCore 0:
  10.5 72.7 all-gather.5
  85.1 49.5 all-gather.7
  136.5 127.2 all-gather.9
  265.6 86.9 all-gather.11
  434.7 27.9 reduce-scatter.6
  466.4 71.2 reduce-scatter.10
  613.2 93.7 reduce-scatter.8
  722.4 44.0 reduce-scatter.4
  769.3 122.0 all-reduce.2

commit v2 on v1

--- a/solution.py
+++ b/solution.py
@@ -22,10 +22,6 @@
     centered = values - jnp.mean(values, axis=-1, keepdims=True)
     spread = jnp.mean(centered * centered, axis=-1, keepdims=True)
     return centered * lax.rsqrt(spread + norm_eps) * norm_gain + norm_shift
-
-
-def exact_gelu(values):
-    return jax.nn.gelu(values, approximate=False)
 
 
 def rows_inner(left, right):
@@ -168,19 +164,64 @@
     )(counts, mixed, grad_attended)
 
 
-def reduce_weight(grad, shards):
+def flip(values, offset):
+    perm = [(rank, rank ^ offset) for rank in range(lax.axis_size("shard"))]
+    return lax.ppermute(values, "shard", perm)
+
+
+def gather_weight(weight):
+    shards, rank, core = lax.axis_size("shard"), lax.axis_index("shard"), lax.axis_index("core")
+    rows, columns = weight.shape
+    halves = weight.reshape(2, rows // 2, columns)
+    mine = lax.dynamic_index_in_dim(halves, core, 0, keepdims=False)
+    full = jnp.zeros((shards, 2, rows // 2, columns), weight.dtype)
+    full = lax.dynamic_update_slice(full, halves[None], (rank, 0, 0, 0))
+    for offset in range(1, shards):
+        piece = flip(mine, offset)
+        partner = lax.ppermute(piece, "core", SWAP)
+        owner = rank ^ offset
+        full = lax.dynamic_update_slice(full, piece[None, None], (owner, core, 0, 0))
+        full = lax.dynamic_update_slice(full, partner[None, None], (owner, 1 - core, 0, 0))
+    return full.reshape(shards * rows, columns)
+
+
+def reduce_weight(grad):
+    shards, rank, core = lax.axis_size("shard"), lax.axis_index("shard"), lax.axis_index("core")
     rows, columns = grad.shape
-    core = lax.axis_index("core")
     halves = grad.reshape(shards, 2, rows // shards // 2, columns)
     own = lax.dynamic_index_in_dim(halves, core, 1, keepdims=False)
     other = lax.dynamic_index_in_dim(halves, 1 - core, 1, keepdims=False).astype(BF)
     received = lax.ppermute(other, "core", SWAP)
-    chip = (own + received.astype(F32)).astype(BF).reshape(rows // 2, columns)
-    group = lax.psum_scatter(chip, "shard", scatter_dimension=0, tiled=True)
-    total = lax.psum(group, "rep")
+    chip = (own + received.astype(F32)).astype(BF)
+    group = lax.dynamic_index_in_dim(chip, rank, 0, keepdims=False).astype(F32)
+    for offset in range(1, shards):
+        piece = lax.dynamic_index_in_dim(chip, rank ^ offset, 0, keepdims=False)
+        group = group + flip(piece, offset).astype(F32)
+    part = lax.psum_scatter(group.astype(BF), "rep", scatter_dimension=0, tiled=True)
+    total = lax.all_gather(part, "rep", axis=0, tiled=True)
     partner = lax.ppermute(total, "core", SWAP)
     pair = jnp.stack([jnp.where(core == 0, total, partner), jnp.where(core == 0, partner, total)])
     return pair.reshape(rows // shards, columns).astype(F32)
+
+
+def columns_to_heads(values):
+    shards, rank = lax.axis_size("shard"), lax.axis_index("shard")
+    wide = values.shape[1] // shards
+    pieces = []
+    for offset in range(shards):
+        piece = lax.dynamic_slice_in_dim(values, (rank ^ offset) * wide, wide, 1)
+        pieces.append(flip(piece, offset) if offset else piece)
+    return jnp.stack(pieces)
+
+
+def heads_to_columns(stacked):
+    shards, rank = lax.axis_size("shard"), lax.axis_index("shard")
+    wide = stacked.shape[2]
+    full = jnp.zeros((stacked.shape[1], shards * wide), stacked.dtype)
+    for offset in range(shards):
+        piece = flip(stacked[offset], offset) if offset else stacked[0]
+        full = lax.dynamic_update_slice(full, piece, (0, (rank ^ offset) * wide))
+    return full
 
 
 def per_device(tokens, counts, w_qkv, w_proj, w_fc1, w_fc2, norm_gains, biases, grad_out):
@@ -199,10 +240,10 @@
     gain_len = norm_gains.shape[0]
     gains_wide = vectors[:, :gain_len].reshape(-1).astype(F32)
     biases_wide = vectors[:, gain_len:].reshape(-1).astype(F32)
-    qkv_full = lax.all_gather(qkv_paired, "shard", axis=0, tiled=True)
-    proj_full = lax.all_gather(w_proj, "shard", axis=0, tiled=True)
-    fc1_full = lax.all_gather(w_fc1, "shard", axis=0, tiled=True)
-    fc2_full = lax.all_gather(w_fc2, "shard", axis=0, tiled=True)
+    qkv_full = gather_weight(qkv_paired)
+    proj_full = gather_weight(w_proj)
+    fc1_full = gather_weight(w_fc1)
+    fc2_full = gather_weight(w_fc2)
 
     inputs = tokens.astype(F32).reshape(row_count, width)
     normed_wide, norm_one_back = jax.vjp(
@@ -213,48 +254,42 @@
     value_bias = biases_wide[3 * width : 4 * width].reshape(pairs, 1, LANES)
     mixed_bias = jnp.concatenate([query_bias, jnp.zeros_like(query_bias), value_bias], axis=1)
     mixed = (times(normed_one, qkv_full) + mixed_bias.reshape(1, 3 * width)).astype(BF)
-    own_heads = lax.all_to_all(
-        mixed.reshape(row_count, shards, -1), "shard", split_axis=1, concat_axis=0
-    )
-    own_heads = own_heads.reshape(shards, images, slot_rows, -1)
-    attended = attend_forward(counts, own_heads)
-    attended = lax.all_to_all(
-        attended.reshape(shards, row_count, -1), "shard", split_axis=0, concat_axis=1
-    ).reshape(row_count, width)
+    own_heads = columns_to_heads(mixed).reshape(shards, images, slot_rows, -1)
+    source_counts = jnp.take(counts, jnp.arange(shards) ^ shard_rank, axis=1)
+    attended = attend_forward(source_counts, own_heads)
+    attended = heads_to_columns(attended.reshape(shards, row_count, -1))
     middle = inputs + times(attended, proj_full) + biases_wide[4 * width : 5 * width]
     normed_mid, norm_two_back = jax.vjp(
         layer_norm, middle, gains_wide[width:], biases_wide[width : 2 * width]
     )
     normed_two = normed_mid.astype(BF)
     before = times(normed_two, fc1_full) + biases_wide[6 * width :]
-    hidden_wide, gelu_back = jax.vjp(exact_gelu, before)
-    hidden = hidden_wide.astype(BF)
+    normal_cdf = 0.5 + 0.5 * lax.erf(before * 0.5**0.5)
+    density = jnp.exp(-0.5 * before * before) * (2.0 * jnp.pi) ** -0.5
+    hidden, gelu_slope = lax.optimization_barrier(
+        ((before * normal_cdf).astype(BF), normal_cdf + before * density)
+    )
     outcome = (middle + times(hidden, fc2_full) + biases_wide[5 * width : 6 * width]) * row_valid
     output = outcome.astype(BF).reshape(shaped)
 
     grad_rows = grad_out.astype(F32).reshape(row_count, width) * row_valid
     grad_branch = grad_rows.astype(BF)
-    grad_fc2 = reduce_weight(rows_inner(hidden, grad_branch), shards)
+    grad_fc2 = reduce_weight(rows_inner(hidden, grad_branch))
     grad_out_bias = jnp.sum(grad_branch, axis=0, dtype=F32)
-    grad_hidden = times_transpose(grad_branch, fc2_full)
-    grad_before = gelu_back(grad_hidden)[0].astype(BF)
-    grad_fc1 = reduce_weight(rows_inner(normed_two, grad_before), shards)
+    grad_before = (times_transpose(grad_branch, fc2_full) * gelu_slope).astype(BF)
+    grad_fc1 = reduce_weight(rows_inner(normed_two, grad_before))
     grad_hidden_bias = jnp.sum(grad_before, axis=0, dtype=F32)
     grad_normed_two = times_transpose(grad_before, fc1_full)
     grad_middle_norm, grad_gain_two, grad_shift_two = norm_two_back(grad_normed_two)
     grad_middle = grad_rows + grad_middle_norm
     grad_branch_one = grad_middle.astype(BF)
-    grad_proj = reduce_weight(rows_inner(attended, grad_branch_one), shards)
+    grad_proj = reduce_weight(rows_inner(attended, grad_branch_one))
     grad_proj_bias = jnp.sum(grad_branch_one, axis=0, dtype=F32)
     grad_attended = times_transpose(grad_branch_one, proj_full).astype(BF)
-    grad_heads = lax.all_to_all(
-        grad_attended.reshape(row_count, shards, -1), "shard", split_axis=1, concat_axis=0
-    ).reshape(shards, images, slot_rows, -1)
-    grad_own = attend_backward(counts, own_heads, grad_heads)
-    grad_mixed = lax.all_to_all(
-        grad_own.reshape(shards, row_count, -1), "shard", split_axis=0, concat_axis=1
-    ).reshape(row_count, 3 * width)
-    grad_qkv = reduce_weight(rows_inner(normed_one, grad_mixed), shards)
+    grad_heads = columns_to_heads(grad_attended).reshape(shards, images, slot_rows, -1)
+    grad_own = attend_backward(source_counts, own_heads, grad_heads)
+    grad_mixed = heads_to_columns(grad_own.reshape(shards, row_count, -1))
+    grad_qkv = reduce_weight(rows_inner(normed_one, grad_mixed))
     grad_qkv = grad_qkv.reshape(-1, pairs, 3, LANES).swapaxes(1, 2).reshape(w_qkv.shape)
     column_sums = jnp.sum(grad_mixed, axis=0, dtype=F32).reshape(pairs, 3, LANES)
     grad_normed_one = times_transpose(grad_mixed, qkv_full)

time: 974 us -> 957 us (0.983)
  blocking collectives: 186 us -> 116 us
  matrix products: 186 us -> 129 us
  waiting for transfers between devices: 257 us -> 303 us
  starting transfers between devices: 12 us -> 46.4 us
  local copies, waits for them, and re-layouts: 122 us -> 141 us
  other arithmetic: 62.6 us -> 76 us
    ppermute x0 -> x48, waiting for transfers between devices: none -> 300 us  [the longest x36 299 us: flip(): return lax.ppermute(values, 'shard', perm)]
    all_to_all x2 -> x0, blocking collectives: 137 us -> none  [the longest x1 92.9 us: per_device(): lax.all_to_all(mixed.reshape(row_count, shards, -1), 'shard', split_axis=...]
    all_to_all x2 -> x0, waiting for transfers between devices: 85.3 us -> none  [the longest x1 69.7 us: per_device(): lax.all_to_all(grad_own.reshape(shards, row_count, -1), 'shard', split_ax...]
    psum x1 -> x0, waiting for transfers between devices: 85.1 us -> none  [reduce_weight(): total = lax.psum(group, 'rep')]
    all_gather x4 -> x2, waiting for transfers between devices: 55.9 us -> 0.01 us  [reduce_weight(): total = lax.all_gather(part, 'rep', axis=0, tiled=True)]
    ppermute x0 -> x48, starting transfers between devices: none -> 45.4 us  [the longest x36 43.9 us: flip(): return lax.ppermute(values, 'shard', perm)]
    all_gather x0 -> x2, blocking collectives: none -> 39.5 us  [reduce_weight(): total = lax.all_gather(part, 'rep', axis=0, tiled=True)]
    dynamic_update_slice x0 -> x36, local copies, waits for them, and re-layouts: none -> 35.8 us  [the longest x12 16.9 us: gather_weight(): lax.dynamic_update_slice(full, piece[None, None], (owner, core, 0, 0))]
  transfers between devices with their start and end apart: 19 -> 62, of which waited for: 7 -> 22; matrix products, arithmetic and copies ran while one was open for 35% -> 27% of each run, Pallas kernels for 13% -> 13%
where the time goes in v2:
time: 957 us; the launch traced here: 952 us
  waiting for transfers between devices  303 us (32%)
  local copies, waits for them, and re-layouts  141 us (15%)
  matrix products  129 us (13%)
  Pallas kernels  125 us (13%)
  blocking collectives  116 us (12%)
  other arithmetic  76 us (8%)
  starting transfers between devices  46.4 us (5%)
  between operations  15.6 us (2%)
    ppermute x36, waiting for transfers between devices, flip(): return lax.ppermute(values, 'shard', perm)  299 us
    pallas_call x1, Pallas kernels, attend_backward(): pl.pallas_call(backward_kernel, grid=(images, pairs), in_specs=[pl.BlockS...  81.6 us
    dot_general x4, matrix products, rows_inner(): lax.dot_general(left, right, (((0,), (0,)), ((), ())), preferred_element_...  44.5 us
    ppermute x36, starting transfers between devices, flip(): return lax.ppermute(values, 'shard', perm)  43.9 us
    dot_general x4, matrix products, times(): return jnp.dot(left, right, preferred_element_type=F32)  43.4 us
    pallas_call x1, Pallas kernels, attend_forward(): pl.pallas_call(forward_kernel, grid=(images, pairs), in_specs=[pl.BlockSp...  43.4 us
    dot_general x4, matrix products, times_transpose(): lax.dot_general(left, right, (((1,), (1,)), ((), ())), preferred_element_...  41.5 us
    psum x1, blocking collectives, per_device(): lax.psum(jnp.concatenate([grad_gains, grad_biases], axis=1), ('rep', 'cor...  40 us
  transfers between devices with their start and end apart: 62, of which 22 were waited for; matrix products, arithmetic and copies ran while one was open for 27% of the time, Pallas kernels for 13%

profile of v2, /device:TPU:0, one launch (start us, length us, event | category | flops | bytes accessed | tf_op | source)
XLA Modules:
  0.0 951.8 jit_solution(7739517411430206070)
XLA Ops:
  29.1 36.5 %all-gather = bf16[12288]{0:T(1024)(128)(2,1)S(1)} all-gather(bf16[3072]{0:T(1024)(128)(2,1)S(1)} %pad_maximum_fusion.7), channel_id=2, replica_groups=mesh['rep'=4,'core'=2,'shard'=4] {'shard'}, dimensions={0}, use_global_device_ids=true | all-gather | bytes 30720 | tf_op jit(solution)/shard_map/all_gather | solution.py:239
  120.7 19.3 %collective-permute-done.24 = bf16[512,1024]{1,0:T(8,128)(2,1)S(1)} collective-permute-done((bf16[512,1024]{1,0:T(8,128)(2,1)}, bf16[512,1024]{1,0:T(8,128)(2,1)S(1)}, u32[]{:S(2)}, u32[]{:S(2)}) %collective-permute-start.24) | collective-permute-done | bytes 1048608 | tf_op jit(solution)/shard_map/ppermute | solution.py:169
  142.6 19.9 %collective-permute-done.18 = bf16[128,4096]{1,0:T(8,128)(2,1)S(1)} collective-permute-done((bf16[128,4096]{1,0:T(8,128)(2,1)}, bf16[128,4096]{1,0:T(8,128)(2,1)S(1)}, u32[]{:S(2)}, u32[]{:S(2)}) %collective-permute-start.18) | collective-permute-done | bytes 1048608 | tf_op jit(solution)/shard_map/ppermute | solution.py:169
  174.4 8.7 add_convert_fusion
  185.1 43.6 %collective-permute-done.26 = bf16[512,1024]{1,0:T(8,128)(2,1)S(1)} collective-permute-done((bf16[512,1024]{1,0:T(8,128)(2,1)S(1)}, bf16[512,1024]{1,0:T(8,128)(2,1)S(1)}, u32[]{:S(2)}, u32[]{:S(2)}) %collective-permute-start.26) | collective-permute-done | bytes 1048608 | tf_op jit(solution)/shard_map/ppermute | solution.py:169
  241.2 22.1 %collective-permute-done.6 = bf16[864,768]{1,0:T(8,128)(2,1)S(1)} collective-permute-done((bf16[864,768]{1,0:T(8,128)(2,1)S(1)}, bf16[864,768]{1,0:T(8,128)(2,1)S(1)}, u32[]{:S(2)}, u32[]{:S(2)}) %collective-permute-start.6) | collective-permute-done | bytes 1327136 | tf_op jit(solution)/shard_map/ppermute | solution.py:169
  263.3 30.9 %collective-permute-done.7 = bf16[864,768]{1,0:T(8,128)(2,1)S(1)} collective-permute-done((bf16[864,768]{1,0:T(8,128)(2,1)S(1)}, bf16[864,768]{1,0:T(8,128)(2,1)S(1)}, u32[]{:S(2)}, u32[]{:S(2)}) %collective-permute-start.7) | collective-permute-done | bytes 1327136 | tf_op jit(solution)/shard_map/ppermute | solution.py:169
  295.0 43.4 %shard_map.152 = bf16[4,4,216,256]{3,2,1,0:T(8,128)(2,1)S(1)} custom-call(s32[4,4]{1,0:T(4,128)S(1)} %select_bitcast_fusion.8.counts_ref, bf16[4,4,216,768]{3,2,1,0:T(8,128)(2,1)S(1)} %pad_maximum_fusion.mixed_ref), custom_call_target="tpu_custom_call" | custom-call | flops 3057647616 | bytes 7962624 | tf_op jit(solution)/shard_map/pallas_call | solution.py:130
  344.4 7.3 collective-permute-done.9
  351.7 8.5 collective-permute-done.10
  365.8 16.9 %fusion.3 = (f32[864,4096]{1,0:T(8,128)}, bf16[864,4096]{1,0:T(8,128)(2,1)}) fusion(f32[4096]{0:T(1024)S(1)} %slice-done.6, bf16[1024,4096]{1,0:T(8,128)(2,1)S(1)} %bitcast.266, f32[864,1024]{1,0:T(8,128)S(1)} %bitcast_add_fusion.3, f32[1024]{0:T(1024)S(1)} %copy-done.67, f32[1024]{0:T(1024)S(1)} %bitcast.307, f32[864]{0:T(1024)S(1)} %fusion.39, ...), kind=kOutput, calls=%fused_computation.5 | convolution fusion | flops 7291994112 | bytes 33196800 | tf_op jit(solution)/shard_map/dot_general | solution.py:36
  382.7 15.4 %convert_reduce_fusion = (f32[4096]{0:T(1024)}, bf16[864,4096]{1,0:T(8,128)(2,1)}) fusion(f32[864,4096]{1,0:T(8,128)} %get-tuple-element.11, bf16[864,1024]{1,0:T(8,128)(2,1)S(1)} %bitcast.284, bf16[4096,1024]{1,0:T(8,128)(2,1)} %bitcast.267), kind=kOutput, calls=%fused_computation.6 | convolution fusion | flops 7261908992 | bytes 31408128 | tf_op jit(solution)/shard_map/dot_general | solution.py:32
  398.1 14.0 %multiply_reduce_fusion = (f32[1024]{0:T(1024)}, f32[864]{0:T(1024)S(1)}, f32[1024]{0:T(1024)}, f32[864,1024]{1,0:T(8,128)S(1)}) fusion(f32[864,1024]{1,0:T(8,128)S(1)} %bitcast_add_fusion.3, f32[864]{0:T(1024)S(1)} %fusion.39, f32[864]{0:T(1024)S(1)} %broadcast_multiply_fusion, f32[1024]{0:T(1024)S(1)} %get-tuple-element.81, f32[1024]{0:T(1024)S(1)} %bitcast.308, ...), kind=kOutput, calls=%fused_computation.44 | convolution fusion | flops 7255716864 | bytes 22571136 | tf_op jit(solution)/shard_map/dot_general | solution.py:32
  424.2 16.9 %dot_general.58 = bf16[4,2,512,864]{2,1,0,3:T(2,128)(2,1)} reshape(bf16[4096,864]{0,1:T(8,128)(2,1)} %bitcast.269) | data formatting | bytes 14155776 | tf_op jit(solution)/shard_map/dot_general | solution.py:28
  441.1 15.2 %fusion.6 = f32[4,2,512,1024]{3,2,1,0:T(8,128)} fusion(bf16[864,1024,1,1]{1,0,3,2:T(8,128)(2,1)S(1)} %bitcast.285, bf16[4,2,512,864]{2,1,0,3:T(2,128)(2,1)} %dot_general.58), kind=kOutput, calls=%fused_computation.18 | convolution fusion | flops 7247757312 | bytes 25624576 | tf_op jit(solution)/shard_map/dot_general | solution.py:28
  464.0 81.6 %shard_map.153 = bf16[4,4,216,768]{3,2,1,0:T(8,128)(2,1)S(1)} custom-call(s32[4,4]{1,0:T(4,128)S(1)} %select_bitcast_fusion.8.counts_ref, bf16[4,4,216,768]{3,2,1,0:T(8,128)(2,1)S(1)} %bitcast.256, bf16[4,4,216,256]{3,2,1,0:T(8,128)(2,1)S(1)} %pad_maximum_fusion.3.grad_ref), custom_call_target="tpu_custom_call" | custom-call | flops 7644119040 | bytes 13271040 | tf_op jit(solution)/shard_map/pallas_call | solution.py:148
  549.6 15.2 %fusion.43 = f32[1024,4096]{1,0:T(8,128)} fusion(bf16[864,4096]{1,0:T(8,128)(2,1)} %get-tuple-element.93, f32[864,1024]{1,0:T(8,128)S(1)} %copy-done.5, f32[1024]{0:T(1024)S(1)} %copy-done.68, f32[1024]{0:T(1024)S(1)} %bitcast.310, f32[864]{0:T(1024)S(1)} %copy-done.56, f32[864]{0:T(1024)S(1)} %copy-done.46, f32[1024]{0:T(1024)S(1)} %get-tuple-element.81), kind=kOutput, calls=%fused_computation.193 | convolution fusion | flops 7253065728 | bytes 27413248 | tf_op jit(solution)/shard_map/dot_general | solution.py:28
  569.1 8.9 collective-permute-done.33
  579.2 28.3 %collective-permute-done.34 = bf16[864,768]{1,0:T(8,128)(2,1)S(1)} collective-permute-done((bf16[864,768]{1,0:T(8,128)(2,1)S(1)}, bf16[864,768]{1,0:T(8,128)(2,1)S(1)}, u32[]{:S(2)}, u32[]{:S(2)}) %collective-permute-start.34) | collective-permute-done | bytes 1327136 | tf_op jit(solution)/shard_map/ppermute | solution.py:169
  610.0 7.8 fusion.52
  622.7 9.7 %fusion.9 = f32[4,2,128,3072]{3,2,1,0:T(8,128)S(1)} fusion(bf16[864,3072]{1,0:T(8,128)(2,1)} %constant_dynamic-update-slice_fusion, bf16[4,2,128,864]{2,1,0,3:T(2,128)(2,1)} %dot_general.53), kind=kOutput, calls=%fused_computation.24 | convolution fusion | flops 5435817984 | bytes 19660800 | tf_op jit(solution)/shard_map/dot_general | solution.py:28
  637.8 6.3 fusion.4
  658.6 12.0 %collective-permute-done.52 = bf16[512,1024]{1,0:T(8,128)(2,1)S(1)} collective-permute-done((bf16[512,1024]{1,0:T(8,128)(2,1)S(1)}, bf16[512,1024]{1,0:T(8,128)(2,1)S(1)}, u32[]{:S(2)}, u32[]{:S(2)}) %collective-permute-start.52) | collective-permute-done | bytes 1048608 | tf_op jit(solution)/shard_map/ppermute | solution.py:169
  670.6 19.7 %collective-permute-done.53 = bf16[512,1024]{1,0:T(8,128)(2,1)S(1)} collective-permute-done((bf16[512,1024]{1,0:T(8,128)(2,1)S(1)}, bf16[512,1024]{1,0:T(8,128)(2,1)S(1)}, u32[]{:S(2)}, u32[]{:S(2)}) %collective-permute-start.53) | collective-permute-done | bytes 1048608 | tf_op jit(solution)/shard_map/ppermute | solution.py:169
  724.0 8.1 fusion.5
  742.5 15.7 %collective-permute-done.38 = bf16[128,3072]{1,0:T(8,128)(2,1)S(1)} collective-permute-done((bf16[128,3072]{1,0:T(8,128)(2,1)S(1)}, bf16[128,3072]{1,0:T(8,128)(2,1)S(1)}, u32[]{:S(2)}, u32[]{:S(2)}) %collective-permute-start.38) | collective-permute-done | bytes 786464 | tf_op jit(solution)/shard_map/ppermute | solution.py:169
  759.7 20.8 %collective-permute-done.47 = bf16[128,4096]{1,0:T(8,128)(2,1)} collective-permute-done((bf16[128,4096]{1,0:T(8,128)(2,1)}, bf16[128,4096]{1,0:T(8,128)(2,1)}, u32[]{:S(2)}, u32[]{:S(2)}) %collective-permute-start.47) | collective-permute-done | bytes 1048608 | tf_op jit(solution)/shard_map/ppermute | solution.py:169
  780.5 20.7 %collective-permute-done.48 = bf16[128,4096]{1,0:T(8,128)(2,1)} collective-permute-done((bf16[128,4096]{1,0:T(8,128)(2,1)}, bf16[128,4096]{1,0:T(8,128)(2,1)}, u32[]{:S(2)}, u32[]{:S(2)}) %collective-permute-start.48) | collective-permute-done | bytes 1048608 | tf_op jit(solution)/shard_map/ppermute | solution.py:169
  805.1 13.5 %multiply_convert_fusion.3 = bf16[864,1024]{1,0:T(8,128)(2,1)} fusion(f32[864,1024]{1,0:T(8,128)} %copy-done.4, f32[864]{0:T(1024)S(1)} %reshape.352, f32[1024]{0:T(1024)S(1)} %copy-done.66, f32[1024]{0:T(1024)S(1)} %get-tuple-element.81, bf16[864,4096]{1,0:T(8,128)(2,1)} %get-tuple-element.10, bf16[4096,1024]{1,0:T(8,128)(2,1)} %bitcast.268), kind=kOutput, calls=%fused_computation.51 | convolution fusion | flops 7252180992 | bytes 20786560 | tf_op jit(solution)/shard_map/dot_general | solution.py:36
  837.1 16.3 %all_gather.21 = bf16[128,1024]{1,0:T(8,128)(2,1)S(1)} all-gather(bf16[32,1024]{1,0:T(8,128)(2,1)} %reduce-scatter.7.cloned.1.call-done), channel_id=1, replica_groups=mesh['rep'=4,'core'=2,'shard'=4] {'rep'}, dimensions={0}, use_global_device_ids=true | all-gather | bytes 327680 | tf_op jit(solution)/shard_map/all_gather | solution.py:201
  853.4 23.2 %all_gather.20 = bf16[128,3072]{1,0:T(8,128)(2,1)S(1)} all-gather(bf16[32,3072]{1,0:T(8,128)(2,1)} %reduce-scatter.5.cloned.1.call-done), channel_id=1, replica_groups=mesh['rep'=4,'core'=2,'shard'=4] {'rep'}, dimensions={0}, use_global_device_ids=true | all-gather | bytes 983040 | tf_op jit(solution)/shard_map/all_gather | solution.py:201
  877.4 40.0 %psum.7 = f32[4,3072]{1,0:T(4,128)S(1)} all-reduce(f32[4,3072]{1,0:T(4,128)S(1)} %pad_maximum_fusion.5), channel_id=1, replica_groups=mesh['rep'=4,'core'=2,'shard'=4] {'rep','core','shard'}, use_global_device_ids=true, to_apply=%region_20.21 | all-reduce | flops 12288 | bytes 98304 | tf_op jit(solution)/shard_map/psum | solution.py:310
  (428 shorter events, 269.9 us)
Async XLA Ops:
  7.2 816.9 %reduce-scatter.11.cloned.1.call-start = ((), (), s32[]{:S(2)}) async-start(), calls=%async_computation.8 | async-start | bytes 1310720 | tf_op jit(solution)/shard_map/reduce_scatter | solution.py:200
  17.6 100.5 %collective-permute-start = (bf16[128,3072]{1,0:T(8,128)(2,1)}, bf16[128,3072]{1,0:T(8,128)(2,1)}, u32[]{:S(2)}, u32[]{:S(2)}) collective-permute-start(bf16[128,3072]{1,0:T(8,128)(2,1)} %bitcast.298), channel_id=1, source_target_pairs={{0,1},{1,0},{2,3},{3,2},{4,5},{5,4},{6,7},{7,6},{8,9},{9,8},{10,11... | collective-permute-start | bytes 2359304 | tf_op jit(solution)/shard_map/ppermute | solution.py:169
  20.6 143.1 %collective-permute-start.2 = (bf16[128,3072]{1,0:T(8,128)(2,1)}, bf16[128,3072]{1,0:T(8,128)(2,1)}, u32[]{:S(2)}, u32[]{:S(2)}) collective-permute-start(bf16[128,3072]{1,0:T(8,128)(2,1)} %bitcast.299), channel_id=1, source_target_pairs={{0,2},{1,3},{2,0},{3,1},{4,6},{5,7},{6,4},{7,5},{8,10},{9,11},{10,... | collective-permute-start | bytes 2359304 | tf_op jit(solution)/shard_map/ppermute | solution.py:169
  22.1 146.3 %collective-permute-start.4 = (bf16[128,3072]{1,0:T(8,128)(2,1)}, bf16[128,3072]{1,0:T(8,128)(2,1)}, u32[]{:S(2)}, u32[]{:S(2)}) collective-permute-start(bf16[128,3072]{1,0:T(8,128)(2,1)} %bitcast.300), channel_id=1, source_target_pairs={{0,3},{1,2},{2,1},{3,0},{4,7},{5,6},{6,5},{7,4},{8,11},{9,10},{10,... | collective-permute-start | bytes 2359304 | tf_op jit(solution)/shard_map/ppermute | solution.py:169
  23.8 72.0 %collective-permute-start.12 = (bf16[128,1024]{1,0:T(8,128)(2,1)}, bf16[128,1024]{1,0:T(8,128)(2,1)}, u32[]{:S(2)}, u32[]{:S(2)}) collective-permute-start(bf16[128,1024]{1,0:T(8,128)(2,1)} %dynamic-slice_bitcast_fusion.14), channel_id=1, source_target_pairs={{0,1},{1,0},{2,3},{3,2},{4,5},{5,4},{6,7},{7,6},{8,9},{9,8},{10,11... | collective-permute-start | bytes 786440 | tf_op jit(solution)/shard_map/ppermute | solution.py:169
  25.7 78.2 %collective-permute-start.14 = (bf16[128,1024]{1,0:T(8,128)(2,1)}, bf16[128,1024]{1,0:T(8,128)(2,1)}, u32[]{:S(2)}, u32[]{:S(2)}) collective-permute-start(bf16[128,1024]{1,0:T(8,128)(2,1)} %dynamic-slice_bitcast_fusion.14), channel_id=1, source_target_pairs={{0,2},{1,3},{2,0},{3,1},{4,6},{5,7},{6,4},{7,5},{8,10},{9,11},{10,... | collective-permute-start | bytes 786440 | tf_op jit(solution)/shard_map/ppermute | solution.py:169
  115.9 46.7 %collective-permute-start.18 = (bf16[128,4096]{1,0:T(8,128)(2,1)}, bf16[128,4096]{1,0:T(8,128)(2,1)S(1)}, u32[]{:S(2)}, u32[]{:S(2)}) collective-permute-start(bf16[128,4096]{1,0:T(8,128)(2,1)} %dynamic-slice_bitcast_fusion.7), channel_id=1, source_target_pairs={{0,1},{1,0},{2,3},{3,2},{4,5},{5,4},{6,7},{7,6},{8,9},{9,8},{10,11... | collective-permute-start | bytes 3145736 | tf_op jit(solution)/shard_map/ppermute | solution.py:169
  118.1 65.7 %collective-permute-start.20 = (bf16[128,4096]{1,0:T(8,128)(2,1)}, bf16[128,4096]{1,0:T(8,128)(2,1)S(1)}, u32[]{:S(2)}, u32[]{:S(2)}) collective-permute-start(bf16[128,4096]{1,0:T(8,128)(2,1)} %dynamic-slice_bitcast_fusion.7), channel_id=1, source_target_pairs={{0,2},{1,3},{2,0},{3,1},{4,6},{5,7},{6,4},{7,5},{8,10},{9,11},{10,... | collective-permute-start | bytes 3145736 | tf_op jit(solution)/shard_map/ppermute | solution.py:169
  140.1 45.0 %collective-permute-start.22 = (bf16[128,4096]{1,0:T(8,128)(2,1)S(1)}, bf16[128,4096]{1,0:T(8,128)(2,1)S(1)}, u32[]{:S(2)}, u32[]{:S(2)}) collective-permute-start(bf16[128,4096]{1,0:T(8,128)(2,1)S(1)} %copy-done.29), channel_id=1, source_target_pairs={{0,3},{1,2},{2,1},{3,0},{4,7},{5,6},{6,5},{7,4},{8,11},{9,10},{10,... | collective-permute-start | bytes 3145736 | tf_op jit(solution)/shard_map/ppermute | solution.py:169
  163.7 65.0 %collective-permute-start.26 = (bf16[512,1024]{1,0:T(8,128)(2,1)S(1)}, bf16[512,1024]{1,0:T(8,128)(2,1)S(1)}, u32[]{:S(2)}, u32[]{:S(2)}) collective-permute-start(bf16[512,1024]{1,0:T(8,128)(2,1)S(1)} %copy-done.28), channel_id=1, source_target_pairs={{0,2},{1,3},{2,0},{3,1},{4,6},{5,7},{6,4},{7,5},{8,10},{9,11},{10,... | collective-permute-start | bytes 3145736 | tf_op jit(solution)/shard_map/ppermute | solution.py:169
  168.4 68.2 %collective-permute-start.28 = (bf16[512,1024]{1,0:T(8,128)(2,1)S(1)}, bf16[512,1024]{1,0:T(8,128)(2,1)S(1)}, u32[]{:S(2)}, u32[]{:S(2)}) collective-permute-start(bf16[512,1024]{1,0:T(8,128)(2,1)S(1)} %copy-done.28), channel_id=1, source_target_pairs={{0,3},{1,2},{2,1},{3,0},{4,7},{5,6},{6,5},{7,4},{8,11},{9,10},{10,... | collective-permute-start | bytes 3145736 | tf_op jit(solution)/shard_map/ppermute | solution.py:169
  173.0 55.7 %collective-permute-start.19 = (bf16[128,4096]{1,0:T(8,128)(2,1)S(1)}, bf16[128,4096]{1,0:T(8,128)(2,1)S(1)}, u32[]{:S(2)}, u32[]{:S(2)}) collective-permute-start(bf16[128,4096]{1,0:T(8,128)(2,1)S(1)} %collective-permute-done.18), channel_id=1, source_target_pairs={{0,4},{4,0},{1,5},{5,1},{2,6},{6,2},{3,7},{7,3},{8,12},{12,8},{9,1... | collective-permute-start | bytes 3145736 | tf_op jit(solution)/shard_map/ppermute | solution.py:181
  183.8 51.1 %collective-permute-start.25 = (bf16[512,1024]{1,0:T(8,128)(2,1)S(1)}, bf16[512,1024]{1,0:T(8,128)(2,1)S(1)}, u32[]{:S(2)}, u32[]{:S(2)}) collective-permute-start(bf16[512,1024]{1,0:T(8,128)(2,1)S(1)} %collective-permute-done.24), channel_id=1, source_target_pairs={{0,4},{4,0},{1,5},{5,1},{2,6},{6,2},{3,7},{7,3},{8,12},{12,8},{9,1... | collective-permute-start | bytes 3145736 | tf_op jit(solution)/shard_map/ppermute | solution.py:181
  185.1 46.2 %collective-permute-start.21 = (bf16[128,4096]{1,0:T(8,128)(2,1)S(1)}, bf16[128,4096]{1,0:T(8,128)(2,1)S(1)}, u32[]{:S(2)}, u32[]{:S(2)}) collective-permute-start(bf16[128,4096]{1,0:T(8,128)(2,1)S(1)} %collective-permute-done.20), channel_id=1, source_target_pairs={{0,4},{4,0},{1,5},{5,1},{2,6},{6,2},{3,7},{7,3},{8,12},{12,8},{9,1... | collective-permute-start | bytes 3145736 | tf_op jit(solution)/shard_map/ppermute | solution.py:181
  234.9 59.4 %collective-permute-start.7 = (bf16[864,768]{1,0:T(8,128)(2,1)S(1)}, bf16[864,768]{1,0:T(8,128)(2,1)S(1)}, u32[]{:S(2)}, u32[]{:S(2)}) collective-permute-start(bf16[864,768]{1,0:T(8,128)(2,1)S(1)} %get-tuple-element.48), channel_id=1, source_target_pairs={{0,2},{1,3},{2,0},{3,1},{4,6},{5,7},{6,4},{7,5},{8,10},{9,11},{10,... | collective-permute-start | bytes 3981320 | tf_op jit(solution)/shard_map/ppermute | solution.py:169
  236.6 57.7 %collective-permute-start.8 = (bf16[864,768]{1,0:T(8,128)(2,1)S(1)}, bf16[864,768]{1,0:T(8,128)(2,1)S(1)}, u32[]{:S(2)}, u32[]{:S(2)}) collective-permute-start(bf16[864,768]{1,0:T(8,128)(2,1)S(1)} %get-tuple-element.47), channel_id=1, source_target_pairs={{0,3},{1,2},{2,1},{3,0},{4,7},{5,6},{6,5},{7,4},{8,11},{9,10},{10,... | collective-permute-start | bytes 3981320 | tf_op jit(solution)/shard_map/ppermute | solution.py:169
  239.1 104.0 %collective-permute-start.29 = (bf16[512,1024]{1,0:T(8,128)(2,1)S(1)}, bf16[512,1024]{1,0:T(8,128)(2,1)S(1)}, u32[]{:S(2)}, u32[]{:S(2)}) collective-permute-start(bf16[512,1024]{1,0:T(8,128)(2,1)S(1)} %collective-permute-done.28), channel_id=1, source_target_pairs={{0,4},{4,0},{1,5},{5,1},{2,6},{6,2},{3,7},{7,3},{8,12},{12,8},{9,1... | collective-permute-start | bytes 3145736 | tf_op jit(solution)/shard_map/ppermute | solution.py:181
  462.4 175.4 %collective-permute-start.51 = (bf16[4,512,1024]{2,1,0:T(8,128)(2,1)}, bf16[4,512,1024]{2,1,0:T(8,128)(2,1)}, u32[]{:S(2)}, u32[]{:S(2)}) collective-permute-start(bf16[4,512,1024]{2,1,0:T(8,128)(2,1)} %fusion.12), channel_id=1, source_target_pairs={{0,4},{4,0},{1,5},{5,1},{2,6},{6,2},{3,7},{7,3},{8,12},{12,8},{9,1... | collective-permute-start | bytes 12582920 | tf_op jit(solution)/shard_map/ppermute | solution.py:194
  547.8 59.7 %collective-permute-start.34 = (bf16[864,768]{1,0:T(8,128)(2,1)S(1)}, bf16[864,768]{1,0:T(8,128)(2,1)S(1)}, u32[]{:S(2)}, u32[]{:S(2)}) collective-permute-start(bf16[864,768]{1,0:T(8,128)(2,1)S(1)} %bitcast.294), channel_id=1, source_target_pairs={{0,2},{1,3},{2,0},{3,1},{4,6},{5,7},{6,4},{7,5},{8,10},{9,11},{10,... | collective-permute-start | bytes 3981320 | tf_op jit(solution)/shard_map/ppermute | solution.py:169
  548.1 60.6 %collective-permute-start.35 = (bf16[864,768]{1,0:T(8,128)(2,1)S(1)}, bf16[864,768]{1,0:T(8,128)(2,1)S(1)}, u32[]{:S(2)}, u32[]{:S(2)}) collective-permute-start(bf16[864,768]{1,0:T(8,128)(2,1)S(1)} %bitcast.292), channel_id=1, source_target_pairs={{0,3},{1,2},{2,1},{3,0},{4,7},{5,6},{6,5},{7,4},{8,11},{9,10},{10,... | collective-permute-start | bytes 3981320 | tf_op jit(solution)/shard_map/ppermute | solution.py:169
  634.8 80.7 %collective-permute-start.36 = (bf16[4,128,3072]{2,1,0:T(8,128)(2,1)}, bf16[4,128,3072]{2,1,0:T(8,128)(2,1)}, u32[]{:S(2)}, u32[]{:S(2)}) collective-permute-start(bf16[4,128,3072]{2,1,0:T(8,128)(2,1)} %fusion.20), channel_id=1, source_target_pairs={{0,4},{4,0},{1,5},{5,1},{2,6},{6,2},{3,7},{7,3},{8,12},{12,8},{9,1... | collective-permute-start | bytes 9437192 | tf_op jit(solution)/shard_map/ppermute | solution.py:194
  644.9 45.5 %collective-permute-start.53 = (bf16[512,1024]{1,0:T(8,128)(2,1)S(1)}, bf16[512,1024]{1,0:T(8,128)(2,1)S(1)}, u32[]{:S(2)}, u32[]{:S(2)}) collective-permute-start(bf16[512,1024]{1,0:T(8,128)(2,1)S(1)} %get-tuple-element.52), channel_id=1, source_target_pairs={{0,2},{1,3},{2,0},{3,1},{4,6},{5,7},{6,4},{7,5},{8,10},{9,11},{10,... | collective-permute-start | bytes 3145736 | tf_op jit(solution)/shard_map/ppermute | solution.py:169
  654.2 69.8 %collective-permute-start.46 = (bf16[4,128,4096]{2,1,0:T(8,128)(2,1)}, bf16[4,128,4096]{2,1,0:T(8,128)(2,1)}, u32[]{:S(2)}, u32[]{:S(2)}) collective-permute-start(bf16[4,128,4096]{2,1,0:T(8,128)(2,1)} %fusion.11), channel_id=1, source_target_pairs={{0,4},{4,0},{1,5},{5,1},{2,6},{6,2},{3,7},{7,3},{8,12},{12,8},{9,1... | collective-permute-start | bytes 12582920 | tf_op jit(solution)/shard_map/ppermute | solution.py:194
  692.3 144.8 %reduce-scatter.7.cloned.1.call-start = ((), (), s32[]{:S(2)}) async-start(), calls=%async_computation.5 | async-start | bytes 327680 | tf_op jit(solution)/shard_map/reduce_scatter | solution.py:200
  715.2 138.2 %reduce-scatter.5.cloned.1.call-start = ((), (), s32[]{:S(2)}) async-start(), calls=%async_computation.4 | async-start | bytes 983040 | tf_op jit(solution)/shard_map/reduce_scatter | solution.py:200
  735.6 44.8 %collective-permute-start.47 = (bf16[128,4096]{1,0:T(8,128)(2,1)}, bf16[128,4096]{1,0:T(8,128)(2,1)}, u32[]{:S(2)}, u32[]{:S(2)}) collective-permute-start(bf16[128,4096]{1,0:T(8,128)(2,1)} %get-tuple-element.53), channel_id=1, source_target_pairs={{0,1},{1,0},{2,3},{3,2},{4,5},{5,4},{6,7},{7,6},{8,9},{9,8},{10,11... | collective-permute-start | bytes 3145736 | tf_op jit(solution)/shard_map/ppermute | solution.py:169
  735.9 65.2 %collective-permute-start.48 = (bf16[128,4096]{1,0:T(8,128)(2,1)}, bf16[128,4096]{1,0:T(8,128)(2,1)}, u32[]{:S(2)}, u32[]{:S(2)}) collective-permute-start(bf16[128,4096]{1,0:T(8,128)(2,1)} %get-tuple-element.55), channel_id=1, source_target_pairs={{0,2},{1,3},{2,0},{3,1},{4,6},{5,7},{6,4},{7,5},{8,10},{9,11},{10,... | collective-permute-start | bytes 3145736 | tf_op jit(solution)/shard_map/ppermute | solution.py:169
  741.0 60.2 %collective-permute-start.49 = (bf16[128,4096]{1,0:T(8,128)(2,1)S(1)}, bf16[128,4096]{1,0:T(8,128)(2,1)}, u32[]{:S(2)}, u32[]{:S(2)}) collective-permute-start(bf16[128,4096]{1,0:T(8,128)(2,1)S(1)} %get-tuple-element.54), channel_id=1, source_target_pairs={{0,3},{1,2},{2,1},{3,0},{4,7},{5,6},{6,5},{7,4},{8,11},{9,10},{10,... | collective-permute-start | bytes 3145736 | tf_op jit(solution)/shard_map/ppermute | solution.py:169
  759.6 117.0 %reduce-scatter.9.cloned.1.call-start = ((), (), s32[]{:S(2)}) async-start(), calls=%async_computation.6 | async-start | bytes 1310720 | tf_op jit(solution)/shard_map/reduce_scatter | solution.py:200
  805.0 114.9 %all-gather.6.cloned.1.call-start = ((), (), s32[]{:S(2)}) async-start(), calls=%async_computation.9 | async-start | bytes 1310720 | tf_op jit(solution)/shard_map/all_gather | solution.py:201
  824.1 97.1 %all-gather.4.cloned.1.call-start = ((), (), s32[]{:S(2)}) async-start(), calls=%async_computation.7 | async-start | bytes 1310720 | tf_op jit(solution)/shard_map/all_gather | solution.py:201
  853.4 65.3 %collective-permute-start.45 = (bf16[128,1024]{1,0:T(8,128)(2,1)S(1)}, bf16[128,1024]{1,0:T(8,128)(2,1)S(1)}, u32[]{:S(2)}, u32[]{:S(2)}) collective-permute-start(bf16[128,1024]{1,0:T(8,128)(2,1)S(1)} %all_gather.21), channel_id=1, source_target_pairs={{0,4},{4,0},{1,5},{5,1},{2,6},{6,2},{3,7},{7,3},{8,12},{12,8},{9,1... | collective-permute-start | bytes 786440 | tf_op jit(solution)/shard_map/ppermute | solution.py:202
  (107 other events, 1627.3 us)
Sparse Core Ops, SparseCore 0:
  692.4 27.6 reduce-scatter.10
  722.5 18.3 reduce-scatter.6
  759.7 23.8 reduce-scatter.4
  805.1 27.5 reduce-scatter.8
  834.2 34.0 all-gather.5
  876.8 27.5 all-gather.3

commit v3 on v2

--- a/solution.py
+++ b/solution.py
@@ -164,9 +164,36 @@
     )(counts, mixed, grad_attended)
 
 
-def flip(values, offset):
-    perm = [(rank, rank ^ offset) for rank in range(lax.axis_size("shard"))]
-    return lax.ppermute(values, "shard", perm)
+def flip(values, offset, axis="shard"):
+    perm = [(rank, rank ^ offset) for rank in range(lax.axis_size(axis))]
+    return lax.ppermute(values, axis, perm)
+
+
+def gather_rows(values, axis):
+    ranks, rank = lax.axis_size(axis), lax.axis_index(axis)
+    full = jnp.zeros((ranks,) + values.shape, values.dtype)
+    origin = (0,) * values.ndim
+    for offset in range(ranks):
+        piece = flip(values, offset, axis) if offset else values
+        full = lax.dynamic_update_slice(full, piece[None], (rank ^ offset,) + origin)
+    return full
+
+
+def scatter_sum(values, axis):
+    ranks, rank = lax.axis_size(axis), lax.axis_index(axis)
+    total = lax.dynamic_index_in_dim(values, rank, 0, keepdims=False).astype(F32)
+    for offset in range(1, ranks):
+        piece = lax.dynamic_index_in_dim(values, rank ^ offset, 0, keepdims=False)
+        total = total + flip(piece, offset, axis).astype(F32)
+    return total
+
+
+def butterfly_sum(values, axis):
+    offset = 1
+    while offset < lax.axis_size(axis):
+        values = values + flip(values, offset, axis)
+        offset *= 2
+    return values
 
 
 def gather_weight(weight):
@@ -185,23 +212,25 @@
     return full.reshape(shards * rows, columns)
 
 
-def reduce_weight(grad):
-    shards, rank, core = lax.axis_size("shard"), lax.axis_index("shard"), lax.axis_index("core")
+def chip_sum(grad):
+    shards, core = lax.axis_size("shard"), lax.axis_index("core")
     rows, columns = grad.shape
     halves = grad.reshape(shards, 2, rows // shards // 2, columns)
     own = lax.dynamic_index_in_dim(halves, core, 1, keepdims=False)
     other = lax.dynamic_index_in_dim(halves, 1 - core, 1, keepdims=False).astype(BF)
     received = lax.ppermute(other, "core", SWAP)
-    chip = (own + received.astype(F32)).astype(BF)
-    group = lax.dynamic_index_in_dim(chip, rank, 0, keepdims=False).astype(F32)
-    for offset in range(1, shards):
-        piece = lax.dynamic_index_in_dim(chip, rank ^ offset, 0, keepdims=False)
-        group = group + flip(piece, offset).astype(F32)
-    part = lax.psum_scatter(group.astype(BF), "rep", scatter_dimension=0, tiled=True)
-    total = lax.all_gather(part, "rep", axis=0, tiled=True)
+    return (own + received.astype(F32)).astype(BF)
+
+
+def finish_weight(chip):
+    replicas, core = lax.axis_size("rep"), lax.axis_index("core")
+    rows, columns = chip.shape[1:]
+    group = scatter_sum(chip, "shard").astype(BF)
+    part = scatter_sum(group.reshape(replicas, rows // replicas, columns), "rep").astype(BF)
+    total = gather_rows(part, "rep").reshape(rows, columns)
     partner = lax.ppermute(total, "core", SWAP)
     pair = jnp.stack([jnp.where(core == 0, total, partner), jnp.where(core == 0, partner, total)])
-    return pair.reshape(rows // shards, columns).astype(F32)
+    return pair.reshape(2 * rows, columns).astype(F32)
 
 
 def columns_to_heads(values):
@@ -236,14 +265,11 @@
     row_valid = (slot_index[None, :] < own_counts).astype(F32).reshape(row_count, 1)
 
     qkv_paired = w_qkv.reshape(-1, 3, pairs, LANES).swapaxes(1, 2).reshape(w_qkv.shape)
-    vectors = lax.all_gather(jnp.concatenate([norm_gains, biases]), "shard", axis=0, tiled=False)
+    vectors = gather_rows(jnp.concatenate([norm_gains, biases]), "shard")
     gain_len = norm_gains.shape[0]
     gains_wide = vectors[:, :gain_len].reshape(-1).astype(F32)
     biases_wide = vectors[:, gain_len:].reshape(-1).astype(F32)
     qkv_full = gather_weight(qkv_paired)
-    proj_full = gather_weight(w_proj)
-    fc1_full = gather_weight(w_fc1)
-    fc2_full = gather_weight(w_fc2)
 
     inputs = tokens.astype(F32).reshape(row_count, width)
     normed_wide, norm_one_back = jax.vjp(
@@ -254,7 +280,13 @@
     value_bias = biases_wide[3 * width : 4 * width].reshape(pairs, 1, LANES)
     mixed_bias = jnp.concatenate([query_bias, jnp.zeros_like(query_bias), value_bias], axis=1)
     mixed = (times(normed_one, qkv_full) + mixed_bias.reshape(1, 3 * width)).astype(BF)
-    own_heads = columns_to_heads(mixed).reshape(shards, images, slot_rows, -1)
+    own_heads, w_proj, w_fc1, w_fc2 = lax.optimization_barrier(
+        (columns_to_heads(mixed), w_proj, w_fc1, w_fc2)
+    )
+    proj_full = gather_weight(w_proj)
+    fc1_full = gather_weight(w_fc1)
+    fc2_full = gather_weight(w_fc2)
+    own_heads = own_heads.reshape(shards, images, slot_rows, -1)
     source_counts = jnp.take(counts, jnp.arange(shards) ^ shard_rank, axis=1)
     attended = attend_forward(source_counts, own_heads)
     attended = heads_to_columns(attended.reshape(shards, row_count, -1))
@@ -274,22 +306,28 @@
 
     grad_rows = grad_out.astype(F32).reshape(row_count, width) * row_valid
     grad_branch = grad_rows.astype(BF)
-    grad_fc2 = reduce_weight(rows_inner(hidden, grad_branch))
+    chip_fc2 = chip_sum(rows_inner(hidden, grad_branch))
     grad_out_bias = jnp.sum(grad_branch, axis=0, dtype=F32)
     grad_before = (times_transpose(grad_branch, fc2_full) * gelu_slope).astype(BF)
-    grad_fc1 = reduce_weight(rows_inner(normed_two, grad_before))
+    chip_fc1 = chip_sum(rows_inner(normed_two, grad_before))
     grad_hidden_bias = jnp.sum(grad_before, axis=0, dtype=F32)
     grad_normed_two = times_transpose(grad_before, fc1_full)
     grad_middle_norm, grad_gain_two, grad_shift_two = norm_two_back(grad_normed_two)
     grad_middle = grad_rows + grad_middle_norm
     grad_branch_one = grad_middle.astype(BF)
-    grad_proj = reduce_weight(rows_inner(attended, grad_branch_one))
+    chip_proj = chip_sum(rows_inner(attended, grad_branch_one))
     grad_proj_bias = jnp.sum(grad_branch_one, axis=0, dtype=F32)
     grad_attended = times_transpose(grad_branch_one, proj_full).astype(BF)
+    grad_attended, chip_fc2, chip_fc1, chip_proj = lax.optimization_barrier(
+        (grad_attended, chip_fc2, chip_fc1, chip_proj)
+    )
+    grad_fc2 = finish_weight(chip_fc2)
+    grad_fc1 = finish_weight(chip_fc1)
+    grad_proj = finish_weight(chip_proj)
     grad_heads = columns_to_heads(grad_attended).reshape(shards, images, slot_rows, -1)
     grad_own = attend_backward(source_counts, own_heads, grad_heads)
     grad_mixed = heads_to_columns(grad_own.reshape(shards, row_count, -1))
-    grad_qkv = reduce_weight(rows_inner(normed_one, grad_mixed))
+    grad_qkv = finish_weight(chip_sum(rows_inner(normed_one, grad_mixed)))
     grad_qkv = grad_qkv.reshape(-1, pairs, 3, LANES).swapaxes(1, 2).reshape(w_qkv.shape)
     column_sums = jnp.sum(grad_mixed, axis=0, dtype=F32).reshape(pairs, 3, LANES)
     grad_normed_one = times_transpose(grad_mixed, qkv_full)
@@ -307,10 +345,8 @@
             grad_hidden_bias,
         ]
     ).reshape(shards, -1)
-    grad_vectors = lax.psum(
-        jnp.concatenate([grad_gains, grad_biases], axis=1), ("rep", "core", "shard")
-    )
-    own_vectors = lax.dynamic_index_in_dim(grad_vectors, shard_rank, 0, keepdims=False)
+    own_vectors = scatter_sum(jnp.concatenate([grad_gains, grad_biases], axis=1), "shard")
+    own_vectors = butterfly_sum(butterfly_sum(own_vectors, "core"), "rep")
     return (
         output,
         grad_tokens,

time: 957 us -> 888 us (0.928)
  blocking collectives: 116 us -> 0 us
  starting transfers between devices: 46.4 us -> 103 us
  waiting for transfers between devices: 303 us -> 316 us
  between operations: 15.6 us -> 2.66 us
    all_gather x3 -> x0, blocking collectives: 75.9 us -> none  [the longest x2 39.5 us: reduce_weight(): total = lax.all_gather(part, 'rep', axis=0, tiled=True)]
    ppermute x44 -> x77, starting transfers between devices: 44.5 us -> 101 us  [the longest x69 100 us: flip(): return lax.ppermute(values, axis, perm)]
    psum x1 -> x0, blocking collectives: 40 us -> none  [per_device(): lax.psum(jnp.concatenate([grad_gains, grad_biases], axis=1), ('rep', 'cor...]
    ppermute x44 -> x77, waiting for transfers between devices: 302 us -> 310 us  [the longest x69 310 us: flip(): return lax.ppermute(values, axis, perm)]
  transfers between devices with their start and end apart: 62 -> 89, of which waited for: 22 -> 36; matrix products, arithmetic and copies ran while one was open for 27% -> 25% of each run, Pallas kernels for 13% -> 14%
where the time goes in v3:
time: 888 us; the launch traced here: 881 us
  waiting for transfers between devices  316 us (36%)
  local copies, waits for them, and re-layouts  137 us (15%)
  Pallas kernels  125 us (14%)
  matrix products  123 us (14%)
  starting transfers between devices  103 us (12%)
  other arithmetic  74.4 us (8%)
    ppermute x69, waiting for transfers between devices, flip(): return lax.ppermute(values, axis, perm)  310 us
    ppermute x69, starting transfers between devices, flip(): return lax.ppermute(values, axis, perm)  100 us
    pallas_call x1, Pallas kernels, attend_backward(): pl.pallas_call(backward_kernel, grid=(images, pairs), in_specs=[pl.BlockS...  81.8 us
    dot_general x4, matrix products, times_transpose(): lax.dot_general(left, right, (((1,), (1,)), ((), ())), preferred_element_...  43.9 us
    pallas_call x1, Pallas kernels, attend_forward(): pl.pallas_call(forward_kernel, grid=(images, pairs), in_specs=[pl.BlockSp...  43.6 us
    dot_general x4, matrix products, rows_inner(): lax.dot_general(left, right, (((0,), (0,)), ((), ())), preferred_element_...  40.2 us
    dot_general x4, matrix products, times(): return jnp.dot(left, right, preferred_element_type=F32)  38.7 us
    convert_element_type x4, other arithmetic, chip_sum(): return (own + received.astype(F32)).astype(BF)  23 us
  transfers between devices with their start and end apart: 89, of which 36 were waited for; matrix products, arithmetic and copies ran while one was open for 25% of the time, Pallas kernels for 14%

profile of v3, /device:TPU:0, one launch (start us, length us, event | category | flops | bytes accessed | tf_op | source)
XLA Modules:
  0.0 881.4 jit_solution(5144775941148260155)
XLA Ops:
  39.3 12.5 %collective-permute-done.7 = bf16[128,3072]{1,0:T(8,128)(2,1)} collective-permute-done((bf16[128,3072]{1,0:T(8,128)(2,1)}, bf16[128,3072]{1,0:T(8,128)(2,1)}, u32[]{:S(2)}, u32[]{:S(2)}) %collective-permute-start.7) | collective-permute-done | bytes 786464 | tf_op jit(solution)/shard_map/ppermute | solution.py:169
  62.0 8.6 add_convert_fusion
  82.6 22.8 %collective-permute-done.9 = bf16[864,768]{1,0:T(8,128)(2,1)} collective-permute-done((bf16[864,768]{1,0:T(8,128)(2,1)}, bf16[864,768]{1,0:T(8,128)(2,1)}, u32[]{:S(2)}, u32[]{:S(2)}) %collective-permute-start.9) | collective-permute-done | bytes 1327136 | tf_op jit(solution)/shard_map/ppermute | solution.py:169
  105.5 29.2 %collective-permute-done.10 = bf16[864,768]{1,0:T(8,128)(2,1)} collective-permute-done((bf16[864,768]{1,0:T(8,128)(2,1)}, bf16[864,768]{1,0:T(8,128)(2,1)}, u32[]{:S(2)}, u32[]{:S(2)}) %collective-permute-start.10) | collective-permute-done | bytes 1327136 | tf_op jit(solution)/shard_map/ppermute | solution.py:169
  143.2 43.6 %shard_map.152 = bf16[4,4,216,256]{3,2,1,0:T(8,128)(2,1)S(1)} custom-call(s32[4,4]{1,0:T(4,128)S(1)} %select_bitcast_fusion.8.counts_ref, bf16[4,4,216,768]{3,2,1,0:T(8,128)(2,1)S(1)} %bitcast.348), custom_call_target="tpu_custom_call" | custom-call | flops 3057647616 | bytes 7962624 | tf_op jit(solution)/shard_map/pallas_call | solution.py:130
  202.6 6.4 collective-permute-done.13
  215.7 25.0 %collective-permute-done.19 = bf16[128,1024]{1,0:T(8,128)(2,1)S(1)} collective-permute-done((bf16[128,1024]{1,0:T(8,128)(2,1)}, bf16[128,1024]{1,0:T(8,128)(2,1)S(1)}, u32[]{:S(2)}, u32[]{:S(2)}) %collective-permute-start.19) | collective-permute-done | bytes 262176 | tf_op jit(solution)/shard_map/ppermute | solution.py:169
  249.2 17.8 %collective-permute-done.21 = bf16[128,4096]{1,0:T(8,128)(2,1)S(1)} collective-permute-done((bf16[128,4096]{1,0:T(8,128)(2,1)S(1)}, bf16[128,4096]{1,0:T(8,128)(2,1)S(1)}, u32[]{:S(2)}, u32[]{:S(2)}) %collective-permute-start.21) | collective-permute-done | bytes 1048608 | tf_op jit(solution)/shard_map/ppermute | solution.py:169
  269.4 14.0 %collective-permute-done.29 = bf16[512,1024]{1,0:T(8,128)(2,1)S(1)} collective-permute-done((bf16[512,1024]{1,0:T(8,128)(2,1)}, bf16[512,1024]{1,0:T(8,128)(2,1)S(1)}, u32[]{:S(2)}, u32[]{:S(2)}) %collective-permute-start.29) | collective-permute-done | bytes 1048608 | tf_op jit(solution)/shard_map/ppermute | solution.py:169
  283.9 20.4 %collective-permute-done.23 = bf16[128,4096]{1,0:T(8,128)(2,1)S(1)} collective-permute-done((bf16[128,4096]{1,0:T(8,128)(2,1)S(1)}, bf16[128,4096]{1,0:T(8,128)(2,1)S(1)}, u32[]{:S(2)}, u32[]{:S(2)}) %collective-permute-start.23) | collective-permute-done | bytes 1048608 | tf_op jit(solution)/shard_map/ppermute | solution.py:169
  310.1 16.8 %fusion.3 = (f32[864,4096]{1,0:T(8,128)}, bf16[864,4096]{1,0:T(8,128)(2,1)}) fusion(f32[4096]{0:T(1024)S(1)} %slice-done.4, bf16[1024,4096]{1,0:T(8,128)(2,1)S(1)} %bitcast.358, f32[864,1024]{1,0:T(8,128)S(1)} %bitcast_add_fusion.3, f32[1024]{0:T(1024)S(1)} %copy-done.72, f32[1024]{0:T(1024)S(1)} %bitcast.408, f32[864]{0:T(1024)S(1)} %fusion.51, ...), kind=kOutput, calls=%fused_computation.5 | convolution fusion | flops 7291994112 | bytes 33196800 | tf_op jit(solution)/shard_map/dot_general | solution.py:36
  332.2 15.5 %convert_reduce_fusion = (f32[4096]{0:T(1024)}, bf16[864,4096]{1,0:T(8,128)(2,1)}) fusion(f32[864,4096]{1,0:T(8,128)} %get-tuple-element.23, bf16[864,1024]{1,0:T(8,128)(2,1)S(1)} %bitcast.384, bf16[4096,1024]{1,0:T(8,128)(2,1)} %bitcast.360), kind=kOutput, calls=%fused_computation.6 | convolution fusion | flops 7261908992 | bytes 31408128 | tf_op jit(solution)/shard_map/dot_general | solution.py:32
  347.8 15.4 %multiply_reduce_fusion = (f32[1024]{0:T(1024)}, f32[864]{0:T(1024)}, f32[1024]{0:T(1024)}, f32[864,1024]{1,0:T(8,128)}) fusion(f32[864,1024]{1,0:T(8,128)S(1)} %bitcast_add_fusion.3, f32[864]{0:T(1024)S(1)} %fusion.51, f32[864]{0:T(1024)S(1)} %broadcast_multiply_fusion, f32[1024]{0:T(1024)S(1)} %copy-done.42, f32[1024]{0:T(1024)S(1)} %bitcast.409, ...), kind=kOutput, calls=%fused_computation.44 | convolution fusion | flops 7255716864 | bytes 22571136 | tf_op jit(solution)/shard_map/dot_general | solution.py:32
  363.2 12.7 %fusion.55 = f32[1024,4096]{1,0:T(8,128)} fusion(bf16[864,4096]{1,0:T(8,128)(2,1)S(1)} %copy-done.75, f32[864,1024]{1,0:T(8,128)S(1)} %bitcast_add_fusion.3, f32[1024]{0:T(1024)S(1)} %copy-done.72, f32[1024]{0:T(1024)S(1)} %bitcast.410, f32[864]{0:T(1024)S(1)} %fusion.51, f32[864]{0:T(1024)S(1)} %broadcast_multiply_fusion, f32[1024]{0:T(1024)S(1)} %copy-done.42), kind=kOutput, calls=%fused_computation.239 | convolution fusion | flops 7253065728 | bytes 27413248 | tf_op jit(solution)/shard_map/dot_general | solution.py:28
  382.1 16.7 %dot_general.52 = bf16[4,2,512,864]{2,1,0,3:T(2,128)(2,1)} reshape(bf16[4096,864]{0,1:T(8,128)(2,1)} %bitcast.362) | data formatting | bytes 14155776 | tf_op jit(solution)/shard_map/dot_general | solution.py:28
  398.8 15.6 %fusion.6 = f32[4,2,512,1024]{3,2,1,0:T(8,128)} fusion(bf16[864,1024,1,1]{1,0,3,2:T(8,128)(2,1)} %bitcast.383, bf16[4,2,512,864]{2,1,0,3:T(2,128)(2,1)} %dot_general.52), kind=kOutput, calls=%fused_computation.18 | convolution fusion | flops 7247757312 | bytes 25624576 | tf_op jit(solution)/shard_map/dot_general | solution.py:28
  414.5 6.3 fusion.11
  439.7 8.2 fusion.4
  447.9 8.5 fusion.5
  460.7 11.2 %multiply_convert_fusion.3 = bf16[864,1024]{1,0:T(8,128)(2,1)} fusion(f32[864,1024]{1,0:T(8,128)S(1)} %copy-done.8, f32[864]{0:T(1024)S(1)} %reshape.385, f32[1024]{0:T(1024)S(1)} %copy-done.71, f32[1024]{0:T(1024)S(1)} %copy-done.42, bf16[864,4096]{1,0:T(8,128)(2,1)S(1)} %bitcast.364, bf16[4096,1024]{1,0:T(8,128)(2,1)} %bitcast.361), kind=kOutput, calls=%fused_computation.51 | convolution fusion | flops 7252180992 | bytes 20786560 | tf_op jit(solution)/shard_map/dot_general | solution.py:36
  508.1 81.8 %shard_map.153 = bf16[4,4,216,768]{3,2,1,0:T(8,128)(2,1)S(1)} custom-call(s32[4,4]{1,0:T(4,128)S(1)} %copy-done.2, bf16[4,4,216,768]{3,2,1,0:T(8,128)(2,1)S(1)} %bitcast.351, bf16[4,4,216,256]{3,2,1,0:T(8,128)(2,1)S(1)} %pad_maximum_fusion.3.grad_ref), custom_call_target="tpu_custom_call" | custom-call | flops 7644119040 | bytes 13271040 | tf_op jit(solution)/shard_map/pallas_call | solution.py:148
  600.7 38.8 %collective-permute-done.74 = bf16[512,1024]{1,0:T(8,128)(2,1)S(1)} collective-permute-done((bf16[512,1024]{1,0:T(8,128)(2,1)S(1)}, bf16[512,1024]{1,0:T(8,128)(2,1)S(1)}, u32[]{:S(2)}, u32[]{:S(2)}) %collective-permute-start.74) | collective-permute-done | bytes 1048608 | tf_op jit(solution)/shard_map/ppermute | solution.py:169
  660.7 7.3 collective-permute-done.77
  677.3 9.1 %collective-permute-done.79 = bf16[128,1024]{1,0:T(8,128)(2,1)S(1)} collective-permute-done((bf16[128,1024]{1,0:T(8,128)(2,1)S(1)}, bf16[128,1024]{1,0:T(8,128)(2,1)S(1)}, u32[]{:S(2)}, u32[]{:S(2)}) %collective-permute-start.79) | collective-permute-done | bytes 262176 | tf_op jit(solution)/shard_map/ppermute | solution.py:169
  688.6 11.9 %collective-permute-done.80 = bf16[128,1024]{1,0:T(8,128)(2,1)S(1)} collective-permute-done((bf16[128,1024]{1,0:T(8,128)(2,1)S(1)}, bf16[128,1024]{1,0:T(8,128)(2,1)S(1)}, u32[]{:S(2)}, u32[]{:S(2)}) %collective-permute-start.80) | collective-permute-done | bytes 262176 | tf_op jit(solution)/shard_map/ppermute | solution.py:169
  705.1 12.2 %collective-permute-done.70 = bf16[32,4096]{1,0:T(8,128)(2,1)S(1)} collective-permute-done((bf16[32,4096]{1,0:T(8,128)(2,1)S(1)}, bf16[32,4096]{1,0:T(8,128)(2,1)S(1)}, u32[]{:S(2)}, u32[]{:S(2)}) %collective-permute-start.70) | collective-permute-done | bytes 262176 | tf_op jit(solution)/shard_map/ppermute | solution.py:169
  719.7 9.7 %fusion.69 = f32[864,1024]{1,0:T(8,128)S(1)} fusion(bf16[864,3072]{1,0:T(8,128)(2,1)S(1)} %constant_dynamic-update-slice_fusion, bf16[1024,3072]{1,0:T(8,128)(2,1)} %bitcast.12), kind=kOutput, calls=%fused_computation.248 | convolution fusion | flops 5435817984 | bytes 15138816 | tf_op jit(solution)/shard_map/dot_general | solution.py:32
  738.2 9.5 %fusion.9 = f32[4,2,128,3072]{3,2,1,0:T(8,128)S(1)} fusion(bf16[864,3072]{1,0:T(8,128)(2,1)} %copy-done.9, bf16[4,2,128,864]{2,1,0,3:T(2,128)(2,1)} %dot_general.58), kind=kOutput, calls=%fused_computation.24 | convolution fusion | flops 5435817984 | bytes 19660800 | tf_op jit(solution)/shard_map/dot_general | solution.py:28
  796.0 15.1 %collective-permute-done.43 = bf16[128,3072]{1,0:T(8,128)(2,1)S(1)} collective-permute-done((bf16[128,3072]{1,0:T(8,128)(2,1)S(1)}, bf16[128,3072]{1,0:T(8,128)(2,1)S(1)}, u32[]{:S(2)}, u32[]{:S(2)}) %collective-permute-start.43) | collective-permute-done | bytes 786464 | tf_op jit(solution)/shard_map/ppermute | solution.py:169
  811.1 15.9 %collective-permute-done.44 = bf16[128,3072]{1,0:T(8,128)(2,1)S(1)} collective-permute-done((bf16[128,3072]{1,0:T(8,128)(2,1)S(1)}, bf16[128,3072]{1,0:T(8,128)(2,1)S(1)}, u32[]{:S(2)}, u32[]{:S(2)}) %collective-permute-start.44) | collective-permute-done | bytes 786464 | tf_op jit(solution)/shard_map/ppermute | solution.py:169
  836.5 7.1 collective-permute-done.47
  852.2 12.8 %collective-permute-done.50 = bf16[32,3072]{1,0:T(8,128)(2,1)S(1)} collective-permute-done((bf16[32,3072]{1,0:T(8,128)(2,1)S(1)}, bf16[32,3072]{1,0:T(8,128)(2,1)S(1)}, u32[]{:S(2)}, u32[]{:S(2)}) %collective-permute-start.50) | collective-permute-done | bytes 196640 | tf_op jit(solution)/shard_map/ppermute | solution.py:169
  (518 shorter events, 320.1 us)
Async XLA Ops:
  73.2 32.2 %collective-permute-start.9 = (bf16[864,768]{1,0:T(8,128)(2,1)}, bf16[864,768]{1,0:T(8,128)(2,1)}, u32[]{:S(2)}, u32[]{:S(2)}) collective-permute-start(bf16[864,768]{1,0:T(8,128)(2,1)} %get-tuple-element.65), channel_id=1, source_target_pairs={{0,1},{1,0},{2,3},{3,2},{4,5},{5,4},{6,7},{7,6},{8,9},{9,8},{10,11... | collective-permute-start | bytes 3981320 | tf_op jit(solution)/shard_map/ppermute | solution.py:169
  74.7 60.0 %collective-permute-start.10 = (bf16[864,768]{1,0:T(8,128)(2,1)}, bf16[864,768]{1,0:T(8,128)(2,1)}, u32[]{:S(2)}, u32[]{:S(2)}) collective-permute-start(bf16[864,768]{1,0:T(8,128)(2,1)} %get-tuple-element.64), channel_id=1, source_target_pairs={{0,2},{1,3},{2,0},{3,1},{4,6},{5,7},{6,4},{7,5},{8,10},{9,11},{10,... | collective-permute-start | bytes 3981320 | tf_op jit(solution)/shard_map/ppermute | solution.py:169
  76.1 58.6 %collective-permute-start.11 = (bf16[864,768]{1,0:T(8,128)(2,1)}, bf16[864,768]{1,0:T(8,128)(2,1)}, u32[]{:S(2)}, u32[]{:S(2)}) collective-permute-start(bf16[864,768]{1,0:T(8,128)(2,1)} %get-tuple-element.63), channel_id=1, source_target_pairs={{0,3},{1,2},{2,1},{3,0},{4,7},{5,6},{6,5},{7,4},{8,11},{9,10},{10,... | collective-permute-start | bytes 3981320 | tf_op jit(solution)/shard_map/ppermute | solution.py:169
  138.7 55.9 %collective-permute-start.15 = (bf16[128,1024]{1,0:T(8,128)(2,1)}, bf16[128,1024]{1,0:T(8,128)(2,1)}, u32[]{:S(2)}, u32[]{:S(2)}) collective-permute-start(bf16[128,1024]{1,0:T(8,128)(2,1)} %dynamic-slice_bitcast_fusion.21), channel_id=1, source_target_pairs={{0,1},{1,0},{2,3},{3,2},{4,5},{5,4},{6,7},{7,6},{8,9},{9,8},{10,11... | collective-permute-start | bytes 786440 | tf_op jit(solution)/shard_map/ppermute | solution.py:169
  139.9 73.2 %collective-permute-start.17 = (bf16[128,1024]{1,0:T(8,128)(2,1)}, bf16[128,1024]{1,0:T(8,128)(2,1)}, u32[]{:S(2)}, u32[]{:S(2)}) collective-permute-start(bf16[128,1024]{1,0:T(8,128)(2,1)} %dynamic-slice_bitcast_fusion.21), channel_id=1, source_target_pairs={{0,2},{1,3},{2,0},{3,1},{4,6},{5,7},{6,4},{7,5},{8,10},{9,11},{10,... | collective-permute-start | bytes 786440 | tf_op jit(solution)/shard_map/ppermute | solution.py:169
  141.8 105.8 %collective-permute-start.27 = (bf16[512,1024]{1,0:T(8,128)(2,1)}, bf16[512,1024]{1,0:T(8,128)(2,1)}, u32[]{:S(2)}, u32[]{:S(2)}) collective-permute-start(bf16[512,1024]{1,0:T(8,128)(2,1)} %dynamic-slice_bitcast_fusion.7), channel_id=1, source_target_pairs={{0,1},{1,0},{2,3},{3,2},{4,5},{5,4},{6,7},{7,6},{8,9},{9,8},{10,11... | collective-permute-start | bytes 3145736 | tf_op jit(solution)/shard_map/ppermute | solution.py:169
  209.0 74.4 %collective-permute-start.29 = (bf16[512,1024]{1,0:T(8,128)(2,1)}, bf16[512,1024]{1,0:T(8,128)(2,1)S(1)}, u32[]{:S(2)}, u32[]{:S(2)}) collective-permute-start(bf16[512,1024]{1,0:T(8,128)(2,1)} %dynamic-slice_bitcast_fusion.7), channel_id=1, source_target_pairs={{0,2},{1,3},{2,0},{3,1},{4,6},{5,7},{6,4},{7,5},{8,10},{9,11},{10,... | collective-permute-start | bytes 3145736 | tf_op jit(solution)/shard_map/ppermute | solution.py:169
  211.5 71.9 %collective-permute-start.31 = (bf16[512,1024]{1,0:T(8,128)(2,1)}, bf16[512,1024]{1,0:T(8,128)(2,1)S(1)}, u32[]{:S(2)}, u32[]{:S(2)}) collective-permute-start(bf16[512,1024]{1,0:T(8,128)(2,1)} %dynamic-slice_bitcast_fusion.7), channel_id=1, source_target_pairs={{0,3},{1,2},{2,1},{3,0},{4,7},{5,6},{6,5},{7,4},{8,11},{9,10},{10,... | collective-permute-start | bytes 3145736 | tf_op jit(solution)/shard_map/ppermute | solution.py:169
  244.5 59.8 %collective-permute-start.23 = (bf16[128,4096]{1,0:T(8,128)(2,1)S(1)}, bf16[128,4096]{1,0:T(8,128)(2,1)S(1)}, u32[]{:S(2)}, u32[]{:S(2)}) collective-permute-start(bf16[128,4096]{1,0:T(8,128)(2,1)S(1)} %copy-done.34), channel_id=1, source_target_pairs={{0,2},{1,3},{2,0},{3,1},{4,6},{5,7},{6,4},{7,5},{8,10},{9,11},{10,... | collective-permute-start | bytes 3145736 | tf_op jit(solution)/shard_map/ppermute | solution.py:169
  247.6 56.7 %collective-permute-start.25 = (bf16[128,4096]{1,0:T(8,128)(2,1)S(1)}, bf16[128,4096]{1,0:T(8,128)(2,1)S(1)}, u32[]{:S(2)}, u32[]{:S(2)}) collective-permute-start(bf16[128,4096]{1,0:T(8,128)(2,1)S(1)} %copy-done.34), channel_id=1, source_target_pairs={{0,3},{1,2},{2,1},{3,0},{4,7},{5,6},{6,5},{7,4},{8,11},{9,10},{10,... | collective-permute-start | bytes 3145736 | tf_op jit(solution)/shard_map/ppermute | solution.py:169
  267.0 37.8 %collective-permute-start.22 = (bf16[128,4096]{1,0:T(8,128)(2,1)S(1)}, bf16[128,4096]{1,0:T(8,128)(2,1)S(1)}, u32[]{:S(2)}, u32[]{:S(2)}) collective-permute-start(bf16[128,4096]{1,0:T(8,128)(2,1)S(1)} %collective-permute-done.21), channel_id=1, source_target_pairs={{0,4},{4,0},{1,5},{5,1},{2,6},{6,2},{3,7},{7,3},{8,12},{12,8},{9,1... | collective-permute-start | bytes 3145736 | tf_op jit(solution)/shard_map/ppermute | solution.py:208
  283.4 43.5 %collective-permute-start.28 = (bf16[512,1024]{1,0:T(8,128)(2,1)}, bf16[512,1024]{1,0:T(8,128)(2,1)S(1)}, u32[]{:S(2)}, u32[]{:S(2)}) collective-permute-start(bf16[512,1024]{1,0:T(8,128)(2,1)} %collective-permute-done.27), channel_id=1, source_target_pairs={{0,4},{4,0},{1,5},{5,1},{2,6},{6,2},{3,7},{7,3},{8,12},{12,8},{9,1... | collective-permute-start | bytes 3145736 | tf_op jit(solution)/shard_map/ppermute | solution.py:208
  283.4 45.6 %collective-permute-start.30 = (bf16[512,1024]{1,0:T(8,128)(2,1)S(1)}, bf16[512,1024]{1,0:T(8,128)(2,1)S(1)}, u32[]{:S(2)}, u32[]{:S(2)}) collective-permute-start(bf16[512,1024]{1,0:T(8,128)(2,1)S(1)} %collective-permute-done.29), channel_id=1, source_target_pairs={{0,4},{4,0},{1,5},{5,1},{2,6},{6,2},{3,7},{7,3},{8,12},{12,8},{9,1... | collective-permute-start | bytes 3145736 | tf_op jit(solution)/shard_map/ppermute | solution.py:208
  381.9 57.7 %collective-permute-start.34 = (bf16[4,128,4096]{2,1,0:T(8,128)(2,1)}, bf16[4,128,4096]{2,1,0:T(8,128)(2,1)}, u32[]{:S(2)}, u32[]{:S(2)}) collective-permute-start(bf16[4,128,4096]{2,1,0:T(8,128)(2,1)} %fusion.12), channel_id=1, source_target_pairs={{0,4},{4,0},{1,5},{5,1},{2,6},{6,2},{3,7},{7,3},{8,12},{12,8},{9,1... | collective-permute-start | bytes 12582920 | tf_op jit(solution)/shard_map/ppermute | solution.py:221
  474.3 31.3 %collective-permute-start.36 = (bf16[864,256]{1,0:T(8,128)(2,1)S(1)}, bf16[864,256]{1,0:T(8,128)(2,1)S(1)}, u32[]{:S(2)}, u32[]{:S(2)}) collective-permute-start(bf16[864,256]{1,0:T(8,128)(2,1)S(1)} %get-tuple-element.83), channel_id=1, source_target_pairs={{0,1},{1,0},{2,3},{3,2},{4,5},{5,4},{6,7},{7,6},{8,9},{9,8},{10,11... | collective-permute-start | bytes 1327112 | tf_op jit(solution)/shard_map/ppermute | solution.py:169
  485.8 112.0 %collective-permute-start.73 = (bf16[512,1024]{1,0:T(8,128)(2,1)}, bf16[512,1024]{1,0:T(8,128)(2,1)}, u32[]{:S(2)}, u32[]{:S(2)}) collective-permute-start(bf16[512,1024]{1,0:T(8,128)(2,1)} %get-tuple-element.66), channel_id=1, source_target_pairs={{0,1},{1,0},{2,3},{3,2},{4,5},{5,4},{6,7},{7,6},{8,9},{9,8},{10,11... | collective-permute-start | bytes 3145736 | tf_op jit(solution)/shard_map/ppermute | solution.py:169
  504.3 88.6 %collective-permute-start.63 = (bf16[128,4096]{1,0:T(8,128)(2,1)}, bf16[128,4096]{1,0:T(8,128)(2,1)}, u32[]{:S(2)}, u32[]{:S(2)}) collective-permute-start(bf16[128,4096]{1,0:T(8,128)(2,1)} %get-tuple-element.69), channel_id=1, source_target_pairs={{0,1},{1,0},{2,3},{3,2},{4,5},{5,4},{6,7},{7,6},{8,9},{9,8},{10,11... | collective-permute-start | bytes 3145736 | tf_op jit(solution)/shard_map/ppermute | solution.py:169
  505.5 88.9 %collective-permute-start.64 = (bf16[128,4096]{1,0:T(8,128)(2,1)}, bf16[128,4096]{1,0:T(8,128)(2,1)}, u32[]{:S(2)}, u32[]{:S(2)}) collective-permute-start(bf16[128,4096]{1,0:T(8,128)(2,1)} %get-tuple-element.71), channel_id=1, source_target_pairs={{0,2},{1,3},{2,0},{3,1},{4,6},{5,7},{6,4},{7,5},{8,10},{9,11},{10,... | collective-permute-start | bytes 3145736 | tf_op jit(solution)/shard_map/ppermute | solution.py:169
  506.4 88.8 %collective-permute-start.65 = (bf16[128,4096]{1,0:T(8,128)(2,1)}, bf16[128,4096]{1,0:T(8,128)(2,1)}, u32[]{:S(2)}, u32[]{:S(2)}) collective-permute-start(bf16[128,4096]{1,0:T(8,128)(2,1)} %get-tuple-element.70), channel_id=1, source_target_pairs={{0,3},{1,2},{2,1},{3,0},{4,7},{5,6},{6,5},{7,4},{8,11},{9,10},{10,... | collective-permute-start | bytes 3145736 | tf_op jit(solution)/shard_map/ppermute | solution.py:169
  507.9 83.3 %collective-permute-start.62 = (bf16[128,1024]{1,0:T(8,128)(2,1)S(1)}, bf16[128,1024]{1,0:T(8,128)(2,1)S(1)}, u32[]{:S(2)}, u32[]{:S(2)}) collective-permute-start(bf16[128,1024]{1,0:T(8,128)(2,1)S(1)} %bitcast.396), channel_id=1, source_target_pairs={{0,4},{4,0},{1,5},{5,1},{2,6},{6,2},{3,7},{7,3},{8,12},{12,8},{9,1... | collective-permute-start | bytes 786440 | tf_op jit(solution)/shard_map/ppermute | solution.py:231
  591.5 48.0 %collective-permute-start.74 = (bf16[512,1024]{1,0:T(8,128)(2,1)S(1)}, bf16[512,1024]{1,0:T(8,128)(2,1)S(1)}, u32[]{:S(2)}, u32[]{:S(2)}) collective-permute-start(bf16[512,1024]{1,0:T(8,128)(2,1)S(1)} %copy-done.35), channel_id=1, source_target_pairs={{0,2},{1,3},{2,0},{3,1},{4,6},{5,7},{6,4},{7,5},{8,10},{9,11},{10,... | collective-permute-start | bytes 3145736 | tf_op jit(solution)/shard_map/ppermute | solution.py:169
  592.9 48.9 %collective-permute-start.75 = (bf16[512,1024]{1,0:T(8,128)(2,1)S(1)}, bf16[512,1024]{1,0:T(8,128)(2,1)S(1)}, u32[]{:S(2)}, u32[]{:S(2)}) collective-permute-start(bf16[512,1024]{1,0:T(8,128)(2,1)S(1)} %get-tuple-element.67), channel_id=1, source_target_pairs={{0,3},{1,2},{2,1},{3,0},{4,7},{5,6},{6,5},{7,4},{8,11},{9,10},{10,... | collective-permute-start | bytes 3145736 | tf_op jit(solution)/shard_map/ppermute | solution.py:169
  594.4 124.4 %collective-permute-start.39 = (bf16[864,768]{1,0:T(8,128)(2,1)S(1)}, bf16[864,768]{1,0:T(8,128)(2,1)S(1)}, u32[]{:S(2)}, u32[]{:S(2)}) collective-permute-start(bf16[864,768]{1,0:T(8,128)(2,1)S(1)} %bitcast.391), channel_id=1, source_target_pairs={{0,1},{1,0},{2,3},{3,2},{4,5},{5,4},{6,7},{7,6},{8,9},{9,8},{10,11... | collective-permute-start | bytes 3981320 | tf_op jit(solution)/shard_map/ppermute | solution.py:169
  597.8 46.4 %collective-permute-start.66 = (bf16[32,4096]{1,0:T(8,128)(2,1)S(1)}, bf16[32,4096]{1,0:T(8,128)(2,1)S(1)}, u32[]{:S(2)}, u32[]{:S(2)}) collective-permute-start(bf16[32,4096]{1,0:T(8,128)(2,1)S(1)} %get-tuple-element.93), channel_id=1, source_target_pairs={{0,8},{8,0},{16,24},{24,16},{1,9},{9,1},{17,25},{25,17},{2,10},{10... | collective-permute-start | bytes 786440 | tf_op jit(solution)/shard_map/ppermute | solution.py:169
  597.8 48.4 %collective-permute-start.67 = (bf16[32,4096]{1,0:T(8,128)(2,1)S(1)}, bf16[32,4096]{1,0:T(8,128)(2,1)S(1)}, u32[]{:S(2)}, u32[]{:S(2)}) collective-permute-start(bf16[32,4096]{1,0:T(8,128)(2,1)S(1)} %get-tuple-element.95), channel_id=1, source_target_pairs={{0,16},{8,24},{16,0},{24,8},{1,17},{9,25},{17,1},{25,9},{2,18},{10... | collective-permute-start | bytes 786440 | tf_op jit(solution)/shard_map/ppermute | solution.py:169
  660.1 59.2 %collective-permute-start.40 = (bf16[864,768]{1,0:T(8,128)(2,1)S(1)}, bf16[864,768]{1,0:T(8,128)(2,1)S(1)}, u32[]{:S(2)}, u32[]{:S(2)}) collective-permute-start(bf16[864,768]{1,0:T(8,128)(2,1)S(1)} %bitcast.390), channel_id=1, source_target_pairs={{0,2},{1,3},{2,0},{3,1},{4,6},{5,7},{6,4},{7,5},{8,10},{9,11},{10,... | collective-permute-start | bytes 3981320 | tf_op jit(solution)/shard_map/ppermute | solution.py:169
  668.1 51.4 %collective-permute-start.41 = (bf16[864,768]{1,0:T(8,128)(2,1)S(1)}, bf16[864,768]{1,0:T(8,128)(2,1)S(1)}, u32[]{:S(2)}, u32[]{:S(2)}) collective-permute-start(bf16[864,768]{1,0:T(8,128)(2,1)S(1)} %bitcast.389), channel_id=1, source_target_pairs={{0,3},{1,2},{2,1},{3,0},{4,7},{5,6},{6,5},{7,4},{8,11},{9,10},{10,... | collective-permute-start | bytes 3981320 | tf_op jit(solution)/shard_map/ppermute | solution.py:169
  717.4 114.6 %collective-permute-start.82 = (bf16[512,1024]{1,0:T(8,128)(2,1)}, bf16[512,1024]{1,0:T(8,128)(2,1)}, u32[]{:S(2)}, u32[]{:S(2)}) collective-permute-start(bf16[512,1024]{1,0:T(8,128)(2,1)} %bitcast.145), channel_id=1, source_target_pairs={{0,4},{4,0},{1,5},{5,1},{2,6},{6,2},{3,7},{7,3},{8,12},{12,8},{9,1... | collective-permute-start | bytes 3145736 | tf_op jit(solution)/shard_map/ppermute | solution.py:231
  754.5 31.1 %collective-permute-start.42 = (bf16[4,128,3072]{2,1,0:T(8,128)(2,1)}, bf16[4,128,3072]{2,1,0:T(8,128)(2,1)}, u32[]{:S(2)}, u32[]{:S(2)}) collective-permute-start(bf16[4,128,3072]{2,1,0:T(8,128)(2,1)} %fusion.20), channel_id=1, source_target_pairs={{0,4},{4,0},{1,5},{5,1},{2,6},{6,2},{3,7},{7,3},{8,12},{12,8},{9,1... | collective-permute-start | bytes 9437192 | tf_op jit(solution)/shard_map/ppermute | solution.py:221
  758.7 35.4 %collective-permute-start.72 = (bf16[128,4096]{1,0:T(8,128)(2,1)}, bf16[128,4096]{1,0:T(8,128)(2,1)}, u32[]{:S(2)}, u32[]{:S(2)}) collective-permute-start(bf16[128,4096]{1,0:T(8,128)(2,1)} %bitcast.128), channel_id=1, source_target_pairs={{0,4},{4,0},{1,5},{5,1},{2,6},{6,2},{3,7},{7,3},{8,12},{12,8},{9,1... | collective-permute-start | bytes 3145736 | tf_op jit(solution)/shard_map/ppermute | solution.py:231
  791.8 35.1 %collective-permute-start.44 = (bf16[128,3072]{1,0:T(8,128)(2,1)S(1)}, bf16[128,3072]{1,0:T(8,128)(2,1)S(1)}, u32[]{:S(2)}, u32[]{:S(2)}) collective-permute-start(bf16[128,3072]{1,0:T(8,128)(2,1)S(1)} %get-tuple-element.74), channel_id=1, source_target_pairs={{0,2},{1,3},{2,0},{3,1},{4,6},{5,7},{6,4},{7,5},{8,10},{9,11},{10,... | collective-permute-start | bytes 2359304 | tf_op jit(solution)/shard_map/ppermute | solution.py:169
  792.7 34.2 %collective-permute-start.45 = (bf16[128,3072]{1,0:T(8,128)(2,1)S(1)}, bf16[128,3072]{1,0:T(8,128)(2,1)S(1)}, u32[]{:S(2)}, u32[]{:S(2)}) collective-permute-start(bf16[128,3072]{1,0:T(8,128)(2,1)S(1)} %get-tuple-element.73), channel_id=1, source_target_pairs={{0,3},{1,2},{2,1},{3,0},{4,7},{5,6},{6,5},{7,4},{8,11},{9,10},{10,... | collective-permute-start | bytes 2359304 | tf_op jit(solution)/shard_map/ppermute | solution.py:169
  (138 other events, 2116.9 us)
